TPU v7x, 32 devices: a whole 2x2x4 slice. The times are simulated.
32 devices in a mesh: dp: 8 (over z, x), tensor: 4 (over y, core).
Axes of the slice: x: 2, y: 2, z: 4, core: 2. Of those that a mesh axis runs over, the one named last changes fastest.
Arguments:
- tokens: bfloat16 [8192, 1024], P(('dp', 'tensor')), may hold values from -6 to 6
- segments: int32 [8, 1024], P('dp'), may hold values from 0 to 3, never falling along the last dimension, each value on 1 to 512 neighbouring positions
- cotangent: bfloat16 [8192, 1024], P(('dp', 'tensor')), may hold values from -6 to 6
- timestep_norm_gain: float32 [1024], replicated, may hold values from 0.5 to 1.5
- ema_alpha: float32 [1024, 16], P('tensor'), may hold values from 0.05 to 0.95
- ema_delta: float32 [1024, 16], P('tensor'), may hold values from 0.05 to 0.95
- ema_theta: float32 [1024, 16], P('tensor'), may hold values from -1 to 1
- ema_beta: float32 [1024, 16], P('tensor'), may hold values from -3 to 3
- eta_real: float32 [1024, 16], P('tensor'), may hold values from -1 to 1
- eta_imag: float32 [1024, 16], P('tensor'), may hold values from -1 to 1
- ema_omega: float32 [1024], P('tensor'), may hold values from -2 to 2
- w_shared: bfloat16 [1024, 256], P('tensor'), may hold values from -0.1875 to 0.1875
- q_gain: float32 [256], replicated, may hold values from 0.5 to 1.5
- q_bias: float32 [256], replicated, may hold values from -2 to 2
- k_gain: float32 [256], replicated, may hold values from 0.5 to 1.5
- w_attgate: bfloat16 [1024, 2048], P(None, 'tensor'), may hold values from -0.1875 to 0.1875
- w_value: bfloat16 [1024, 2048], P(None, 'tensor'), may hold values from -0.1875 to 0.1875
- w_attout: bfloat16 [2048, 1024], P('tensor'), may hold values from -0.75 to 0.75
- rms_gain: float32 [1024], replicated, may hold values from 0.5 to 1.5
- w_gate: bfloat16 [1024, 2560], P(None, 'tensor'), may hold values from -0.1875 to 0.1875
- w_up: bfloat16 [1024, 2560], P(None, 'tensor'), may hold values from -0.1875 to 0.1875
- w_down: bfloat16 [2560, 1024], P('tensor'), may hold values from -0.25 to 0.25
Outputs:
- output: bfloat16 [8192, 1024], P(('dp', 'tensor'))
- grad_tokens: bfloat16 [8192, 1024], P(('dp', 'tensor'))
- grad_norm_gain: float32 [1024], replicated
- grad_alpha: float32 [1024, 16], P('tensor')
- grad_delta: float32 [1024, 16], P('tensor')
- grad_theta: float32 [1024, 16], P('tensor')
- grad_beta: float32 [1024, 16], P('tensor')
- grad_eta_real: float32 [1024, 16], P('tensor')
- grad_eta_imag: float32 [1024, 16], P('tensor')
- grad_omega: float32 [1024], P('tensor')
- grad_shared: float32 [1024, 256], P('tensor')
- grad_q_gain: float32 [256], replicated
- grad_q_bias: float32 [256], replicated
- grad_k_gain: float32 [256], replicated
- grad_attgate: float32 [1024, 2048], P(None, 'tensor')
- grad_value: float32 [1024, 2048], P(None, 'tensor')
- grad_attout: float32 [2048, 1024], P('tensor')
- grad_rms_gain: float32 [1024], replicated
- grad_gate: float32 [1024, 2560], P(None, 'tensor')
- grad_up: float32 [1024, 2560], P(None, 'tensor')
- grad_down: float32 [2560, 1024], P('tensor')
Inputs may be any that keep to these rules, and one draw needn't show every extreme that they name: `segments`: within each row segment numbers never fall; each of the 4 documents has 1 to 512 tokens and one has exactly 512.
All inputs are finite; a program needn't handle non-finite values.
Results may differ from a plain program's by a relative error of at most 0.017.
Values may be sent and summed in bfloat16 or wider, within the bound.
A program may use at most 256 MiB of HBM per device.

v0:
```python
import math

import jax
import jax.numpy as jnp
from jax import lax
from jax.sharding import PartitionSpec as P

epsilon = 1e-05
masked_score = -1000000000.0
decay_span = 64
score_rows = 512
highest = lax.Precision.HIGHEST


def plain(left, right):
    return jnp.dot(left, right, preferred_element_type=jnp.float32)


def cross(left, right):
    return lax.dot_general(
        left, right, (((1,), (1,)), ((), ())), preferred_element_type=jnp.float32
    )


def inner(left, right):
    return lax.dot_general(
        left, right, (((0,), (0,)), ((), ())), preferred_element_type=jnp.float32
    )


def inner_exact(left, right):
    return lax.dot_general(
        left, right, (((0,), (0,)), ((), ())), precision=highest, preferred_element_type=jnp.float32
    )


def swish_slope(value):
    sigma = jax.nn.sigmoid(value)
    return sigma * (1.0 + value * (1.0 - sigma))


def decay_filter(
    signal, seg_row, ema_alpha, ema_delta, ema_theta, ema_beta, eta_real, eta_imag, ema_omega
):
    length, channels = signal.shape
    span = min(decay_span, length)
    blocks = length // span
    magnitude = (1.0 - ema_alpha * ema_delta).T[None]
    angle = ema_theta.T[None]
    powers = jnp.arange(span + 1, dtype=jnp.float32)[:, None, None]
    radius = jnp.exp(powers * jnp.log(magnitude))
    power_real = radius * jnp.cos(powers * angle)
    power_imag = radius * jnp.sin(powers * angle)
    weight_real = eta_real.T[None]
    weight_imag = eta_imag.T[None]
    scaled = (ema_alpha * ema_beta).T[None]
    coef_real = weight_real * power_real - weight_imag * power_imag
    coef_imag = weight_real * power_imag + weight_imag * power_real
    kernel = jnp.sum(scaled * coef_real[:span], axis=1)
    lags = jnp.arange(span)[:, None] - jnp.arange(span)[None, :]
    picker = (lags[:, :, None] == jnp.arange(span)[None, None, :]).astype(jnp.float32)
    toeplitz = jnp.einsum("tsl,lc->tsc", picker, kernel, precision=highest)
    entry_real = coef_real[1:]
    entry_imag = coef_imag[1:]
    exit_real = (scaled * power_real[:span])[::-1]
    exit_imag = (scaled * power_imag[:span])[::-1]
    whole_real = power_real[span]
    whole_imag = power_imag[span]

    def one_block(state, entry):
        state_real, state_imag, last_seg = state
        column, seg_block = entry
        same_doc = (seg_block[:, None] == seg_block[None, :]).astype(jnp.float32)
        local_part = jnp.einsum(
            "tsc,sc->tc", toeplitz * same_doc[:, :, None], column, precision=highest
        )
        carried = jnp.sum(entry_real * state_real[None] - entry_imag * state_imag[None], axis=1)
        joined = (seg_block == last_seg).astype(jnp.float32)[:, None]
        tail_seg = seg_block[span - 1]
        tail_input = column * (seg_block == tail_seg).astype(jnp.float32)[:, None]
        keep_flag = (tail_seg == last_seg).astype(jnp.float32)
        next_real = keep_flag * (whole_real * state_real - whole_imag * state_imag) + jnp.einsum(
            "snc,sc->nc", exit_real, tail_input, precision=highest
        )
        next_imag = keep_flag * (whole_real * state_imag + whole_imag * state_real) + jnp.einsum(
            "snc,sc->nc", exit_imag, tail_input, precision=highest
        )
        return ((next_real, next_imag, tail_seg), local_part + joined * carried)

    zero_state = jnp.zeros(whole_real.shape, jnp.float32)
    initial = (zero_state, zero_state, jnp.int32(-1))
    _, pieces = lax.scan(
        jax.checkpoint(one_block),
        initial,
        (signal.reshape(blocks, span, channels), seg_row.reshape(blocks, span)),
    )
    return pieces.reshape(length, channels) + ema_omega * signal


def on_device(
    tokens,
    segments,
    cotangent,
    timestep_norm_gain,
    ema_alpha,
    ema_delta,
    ema_theta,
    ema_beta,
    eta_real,
    eta_imag,
    ema_omega,
    w_shared,
    q_gain,
    q_bias,
    k_gain,
    w_attgate,
    w_value,
    w_attout,
    rms_gain,
    w_gate,
    w_up,
    w_down,
):
    full_tokens, full_cot = (
        lax.all_gather(tokens, "tensor", axis=0, tiled=True),
        lax.all_gather(cotangent, "tensor", axis=0, tiled=True),
    )
    seg_row = segments[0]
    length, width = full_tokens.shape
    shared_portion = tokens.shape[0]
    first_moment = lax.axis_index("tensor") * shared_portion
    channels = ema_alpha.shape[0]
    offset = lax.axis_index("tensor") * channels
    places = jnp.arange(length)
    allowed = (seg_row[:, None] == seg_row[None, :]) & (places[:, None] >= places[None, :])
    weights = allowed.astype(jnp.float32)
    layer_inputs = full_tokens.astype(jnp.float32)
    counts = jnp.sum(weights, axis=1) * width
    first_sum = jnp.dot(weights, jnp.sum(layer_inputs, axis=1), precision=highest)
    second_sum = jnp.dot(weights, jnp.sum(layer_inputs * layer_inputs, axis=1), precision=highest)
    running_mean = first_sum / counts
    inverse_deviation = lax.rsqrt(second_sum / counts - running_mean * running_mean + epsilon)
    standardized_input = (layer_inputs - running_mean[:, None]) * inverse_deviation[:, None]
    normed_output = standardized_input * timestep_norm_gain
    normed_low = normed_output.astype(jnp.bfloat16)
    local_in = lax.dynamic_slice_in_dim(normed_output, offset, channels, 1)

    def run_filter(
        signal, alpha_part, delta_part, theta_part, beta_part, real_part, imag_part, omega_part
    ):
        return decay_filter(
            signal,
            seg_row,
            alpha_part,
            delta_part,
            theta_part,
            beta_part,
            real_part,
            imag_part,
            omega_part,
        )

    filtered, filter_pull = jax.vjp(
        run_filter,
        local_in,
        ema_alpha,
        ema_delta,
        ema_theta,
        ema_beta,
        eta_real,
        eta_imag,
        ema_omega,
    )
    mixed_local = jax.nn.silu(filtered).astype(jnp.bfloat16)
    mixed = lax.all_gather(mixed_local, "tensor", axis=1, tiled=True)
    shared = lax.psum(plain(mixed_local, w_shared), "tensor")
    value_pre = plain(normed_low, w_value)
    values = jax.nn.silu(value_pre).astype(jnp.bfloat16)
    gate_pre = plain(mixed, w_attgate)
    gate_act = jax.nn.silu(gate_pre)
    queries = (shared * q_gain + q_bias).astype(jnp.bfloat16)
    keys = (shared * k_gain).astype(jnp.bfloat16)
    scale = 1.0 / math.sqrt(queries.shape[1])
    block = min(score_rows, length)
    count_blocks = length // block
    attended_parts = []
    log_totals = []
    for index in range(count_blocks):
        rows = slice(index * block, (index + 1) * block)
        limit = length
        scores = jnp.where(allowed[rows, :limit], cross(queries[rows], keys) * scale, masked_score)
        peak = jnp.max(scores, axis=1, keepdims=True)
        expo = jnp.exp(scores - peak)
        total = jnp.sum(expo, axis=1, keepdims=True)
        probs = (expo / total).astype(jnp.bfloat16)
        attended_parts.append(plain(probs, values))
        log_totals.append(peak + jnp.log(total))
    attended = jnp.concatenate(attended_parts, axis=0)
    product = (attended * gate_act).astype(jnp.bfloat16)
    branch = lax.psum(plain(product, w_attout), "tensor")
    resid = layer_inputs + branch
    scale_rms = lax.rsqrt(jnp.mean(resid * resid, axis=1, keepdims=True) + epsilon)
    resid_hat = resid * scale_rms
    resid_low = (resid_hat * rms_gain).astype(jnp.bfloat16)
    own_resid = lax.dynamic_slice_in_dim(resid, first_moment, shared_portion, 0)
    own_hat = lax.dynamic_slice_in_dim(resid_hat, first_moment, shared_portion, 0)
    own_scale = lax.dynamic_slice_in_dim(scale_rms, first_moment, shared_portion, 0)
    gate = plain(resid_low, w_gate)
    up_proj = plain(resid_low, w_up)
    gate_silu = jax.nn.silu(gate)
    hidden = (gate_silu * up_proj).astype(jnp.bfloat16)
    ffn_share = lax.psum_scatter(plain(hidden, w_down), "tensor", scatter_dimension=0, tiled=True)
    output = (own_resid + ffn_share).astype(jnp.bfloat16)
    grad_down = inner(hidden, full_cot)
    d_hidden = cross(full_cot, w_down)
    d_gate = (d_hidden * up_proj * swish_slope(gate)).astype(jnp.bfloat16)
    d_up = (d_hidden * gate_silu).astype(jnp.bfloat16)
    grad_gate = inner(resid_low, d_gate)
    grad_up = inner(resid_low, d_up)
    d_resid_low = lax.psum_scatter(
        cross(d_gate, w_gate) + cross(d_up, w_up), "tensor", scatter_dimension=0, tiled=True
    )
    d_hat = d_resid_low * rms_gain
    rms_part = jnp.sum(d_resid_low * own_hat, axis=0)
    d_resid = cotangent.astype(jnp.float32) + own_scale * (
        d_hat - own_hat * jnp.mean(d_hat * own_hat, axis=1, keepdims=True)
    )
    d_branch = lax.all_gather(d_resid.astype(jnp.bfloat16), "tensor", axis=0, tiled=True)
    grad_attout = inner(product, d_branch)
    d_product = cross(d_branch, w_attout)
    d_attended = (d_product * gate_act).astype(jnp.bfloat16)
    d_gate_pre = (d_product * attended * swish_slope(gate_pre)).astype(jnp.bfloat16)
    d_values = jnp.zeros(values.shape, jnp.float32)
    d_keys = jnp.zeros(keys.shape, jnp.float32)
    keys_wide = keys.astype(jnp.float32)
    query_parts = []
    for index in range(count_blocks):
        rows = slice(index * block, (index + 1) * block)
        limit = length
        scores = jnp.where(allowed[rows, :limit], cross(queries[rows], keys) * scale, masked_score)
        probs_wide = jnp.exp(scores - log_totals[index])
        probs = probs_wide.astype(jnp.bfloat16)
        d_probs = cross(d_attended[rows], values)
        d_scores = (
            probs_wide * (d_probs - jnp.sum(probs_wide * d_probs, axis=1, keepdims=True)) * scale
        )
        query_parts.append(
            jnp.dot(d_scores, keys_wide, precision=highest, preferred_element_type=jnp.float32)
        )
        d_keys = d_keys.at[:limit].add(inner_exact(d_scores, queries[rows].astype(jnp.float32)))
        d_values = d_values.at[:limit].add(inner(probs, d_attended[rows]))
    d_queries = jnp.concatenate(query_parts, axis=0)
    shared_part = d_queries * q_gain + d_keys * k_gain
    affine_part = jnp.stack(
        [
            jnp.sum(d_queries * shared, axis=0),
            jnp.sum(d_queries, axis=0),
            jnp.sum(d_keys * shared, axis=0),
        ]
    )
    d_shared, affine_sums = lax.psum((shared_part, affine_part), "tensor")
    d_shared_low = d_shared.astype(jnp.bfloat16)
    grad_shared = inner(mixed_local, d_shared_low)
    d_value_pre = (d_values * swish_slope(value_pre)).astype(jnp.bfloat16)
    grad_value = inner(normed_low, d_value_pre)
    grad_attgate = inner(mixed, d_gate_pre)
    d_mixed = lax.psum_scatter(
        cross(d_gate_pre, w_attgate), "tensor", scatter_dimension=1, tiled=True
    ) + cross(d_shared_low, w_shared)
    d_filtered = d_mixed * swish_slope(filtered)
    d_signal, grad_alpha, grad_delta, grad_theta, grad_beta, grad_real, grad_imag, grad_omega = (
        filter_pull(d_filtered)
    )
    normed_gradient = cross(d_value_pre, w_value)
    current = lax.dynamic_slice_in_dim(normed_gradient, offset, channels, 1)
    normed_gradient = lax.dynamic_update_slice_in_dim(
        normed_gradient, current + d_signal, offset, 1
    )
    normed_gradient = lax.psum_scatter(normed_gradient, "tensor", scatter_dimension=0, tiled=True)
    own_tokens = tokens.astype(jnp.float32)
    local_mean = lax.dynamic_slice_in_dim(running_mean, first_moment, shared_portion, 0)
    local_inverse_deviation = lax.dynamic_slice_in_dim(
        inverse_deviation, first_moment, shared_portion, 0
    )
    local_counts = lax.dynamic_slice_in_dim(counts, first_moment, shared_portion, 0)
    local_standardized = lax.dynamic_slice_in_dim(
        standardized_input, first_moment, shared_portion, 0
    )
    standardized_gradient = normed_gradient * timestep_norm_gain
    norm_portion = jnp.sum(normed_gradient * local_standardized, axis=0)
    centered_values = own_tokens - local_mean[:, None]
    variance_gradient = (
        -0.5
        * local_inverse_deviation
        * local_inverse_deviation
        * local_inverse_deviation
        * jnp.sum(standardized_gradient * centered_values, axis=1)
    )
    first_gradient = (
        -local_inverse_deviation * jnp.sum(standardized_gradient, axis=1)
        - 2.0 * local_mean * variance_gradient
    ) / local_counts
    d_second = variance_gradient / local_counts
    spread = lax.dynamic_update_slice_in_dim(
        jnp.zeros((2, length), jnp.float32), jnp.stack([first_gradient, d_second]), first_moment, 1
    )
    spread, gain_sums = lax.psum((spread, jnp.stack([norm_portion, rms_part])), "tensor")
    columns = lax.dynamic_slice_in_dim(weights, first_moment, shared_portion, 1)
    pulled_back = jnp.dot(spread, columns, precision=highest, preferred_element_type=jnp.float32)
    d_tokens = (
        d_resid
        + standardized_gradient * local_inverse_deviation[:, None]
        + pulled_back[0][:, None]
        + 2.0 * own_tokens * pulled_back[1][:, None]
    )
    summed_all = lax.psum(
        (
            gain_sums[0],
            grad_alpha,
            grad_delta,
            grad_theta,
            grad_beta,
            grad_real,
            grad_imag,
            grad_omega,
            grad_shared,
            affine_sums[0],
            affine_sums[1],
            affine_sums[2],
            grad_attgate,
            grad_value,
            grad_attout,
            gain_sums[1],
            grad_gate,
            grad_up,
            grad_down,
        ),
        "dp",
    )
    summed = summed_all[:16]
    final_gate, final_up, final_down = (summed_all[16], summed_all[17], summed_all[18])
    return (
        output,
        d_tokens.astype(jnp.bfloat16),
        summed[0],
        summed[1],
        summed[2],
        summed[3],
        summed[4],
        summed[5],
        summed[6],
        summed[7],
        summed[8],
        summed[9],
        summed[10],
        summed[11],
        summed[12],
        summed[13],
        summed[14],
        summed[15],
        final_gate,
        final_up,
        final_down,
    )


def solution(mesh):
    placed = (
        P(("dp", "tensor"), None),
        P("dp", None),
        P(("dp", "tensor"), None),
        P(),
        P("tensor", None),
        P("tensor", None),
        P("tensor", None),
        P("tensor", None),
        P("tensor", None),
        P("tensor", None),
        P("tensor"),
        P("tensor", None),
        P(),
        P(),
        P(),
        P(None, "tensor"),
        P(None, "tensor"),
        P("tensor", None),
        P(),
        P(None, "tensor"),
        P(None, "tensor"),
        P("tensor", None),
    )
    return jax.shard_map(
        on_device,
        mesh=mesh,
        in_specs=placed,
        out_specs=(
            P(("dp", "tensor"), None),
            P(("dp", "tensor"), None),
            P(),
            P("tensor", None),
            P("tensor", None),
            P("tensor", None),
            P("tensor", None),
            P("tensor", None),
            P("tensor", None),
            P("tensor"),
            P("tensor", None),
            P(),
            P(),
            P(),
            P(None, "tensor"),
            P(None, "tensor"),
            P("tensor", None),
            P(),
            P(None, "tensor"),
            P(None, "tensor"),
            P("tensor", None),
        ),
        check_vma=False,
    )
```

profile of v0, /device:TPU:0, one launch (start us, length us, event | category | flops | bytes accessed | tf_op | source)
XLA Modules:
  0.0 1581.4 jit_solution(5881037829061456138)
XLA Ops:
  8.9 4.7 multiply_subtract_fusion
  25.1 9.9 all-gather.5.cloned.1.call-done
  47.4 224.6 %while.64 = (s32[]{:T(128)}, f32[16,256]{1,0:T(8,128)S(1)}, f32[16,256]{1,0:T(8,128)}, s32[]{:T(128)}, f32[16,64,256]{2,1,0:T(8,128)}, /*index=5*/f32[16,16,256]...) while((s32[]{:T(128)}, f32[16,256]{1,0:T(8,128)S(1)}, ...), condition=%wide.region_6.7_spmd.clone, body=%wide.region_4.6_spmd.clone.sunk | while | flops 5308677 | bytes 9440505 | solution.py:92
  279.7 5.4 fusion.7
  285.1 28.4 %all-reduce.16.cloned.1.call-done = f32[1024,256]{1,0:T(8,128)} async-done(((f32[1024,256]{1,0:T(8,128)}), f32[1024,256]{1,0:T(8,128)}) %all-reduce.16.cloned.1.call-update) | async-done | bytes 1048592 | tf_op jit(solution)/shard_map/psum | solution.py:176
  317.1 4.3 online-softmax
  324.5 4.4 online-softmax.1
  329.0 10.0 all-gather.7.cloned.1.call-done
  339.0 5.3 multiply_convert_fusion.7
  349.6 84.6 %all-reduce.18.cloned.1.call-done = f32[1024,1024]{1,0:T(8,128)} async-done(((f32[1024,1024]{1,0:T(8,128)}), f32[1024,1024]{1,0:T(8,128)}) %all-reduce.18.cloned.1.call-update) | async-done | bytes 4194320 | tf_op jit(solution)/shard_map/psum | solution.py:200
  447.5 10.9 all-gather.9.cloned.1.call-done
  458.4 6.8 multiply_convert_fusion.1
  471.5 44.5 %reduce-scatter.7.cloned.1.call-done = f32[256,1024]{1,0:T(8,128)} async-done(((f32[1024,1024]{1,0:T(8,128)}), f32[256,1024]{1,0:T(8,128)}) %reduce-scatter.7.cloned.1.call-update) | async-done | bytes 1048592 | tf_op jit(solution)/shard_map/reduce_scatter | solution.py:220
  520.5 22.7 %all-gather.11.cloned.1.call-done = bf16[1024,1024]{1,0:T(8,128)(2,1)} async-done(((bf16[256,1024]{1,0:T(8,128)(2,1)}), bf16[1024,1024]{1,0:T(8,128)(2,1)}) %all-gather.11.cloned.1.call-update) | async-done | bytes 2097168 | tf_op jit(solution)/shard_map/all_gather | solution.py:228
  543.2 6.2 multiply_convert_fusion.4
  579.5 35.7 %all-reduce.23 = bf16[1024,256]{1,0:T(8,128)(2,1)} all-reduce(f32[1024,256]{1,0:T(8,128)S(1)} %get-tuple-element.1005), channel_id=1, replica_groups=mesh['dp'=8,'tensor'=4] {'tensor'}, use_global_device_ids=true, to_apply=%region_20.21 | all-reduce | flops 262144 | bytes 1572864 | tf_op jit(solution)/shard_map/psum | solution.py:261
  615.2 5.1 multiply_convert_fusion.5
  628.9 327.6 %while.65 = (s32[]{:T(128)}, f32[64,64,256]{2,1,0:T(8,128)}, f32[64,16,256]{2,1,0:T(8,128)}, f32[64,16,256]{2,1,0:T(8,128)}, f32[16,256]{1,0:T(8,128)S(1)}, /*in...) while((s32[]{:T(128)}, f32[64,64,256]{2,1,0:T(8,128)}, ...), condition=%wide.region_24.25_spmd.clone, body=%wide.region_21.24_spmd.clone.sunk | while | flops 12726534 | bytes 43928460 | solution.py:92
  653.0 4.2 bitcast_add_fusion.14
  673.6 4.2 bitcast_add_fusion.14
  694.3 4.2 bitcast_add_fusion.14
  735.6 4.2 bitcast_add_fusion.14
  777.0 4.2 bitcast_add_fusion.14
  818.3 4.2 bitcast_add_fusion.14
  859.6 4.2 bitcast_add_fusion.14
  901.0 4.2 bitcast_add_fusion.14
  962.3 4.6 fusion.88
  985.7 4.3 fusion.13
  994.7 5.1 multiply_reduce_fusion.11
  1009.2 10.3 all-reduce.9
  1024.6 440.0 %all-reduce.22.cloned.1.call-done = (f32[256,256]{1,0:T(8,128)}, f32[1024,512]{1,0:T(8,128)}, f32[1024,512]{1,0:T(8,128)}, f32[512,1024]{1,0:T(8,128)}, f32[1024...) async-done(((f32[256,256]{1,0:T(8,128)}, f32[1024,512]{1,0:T(8,128)}, f32[1024,512]{1,0:T(8,128)}, f32[512,1024]{1,0:T(8,128)}, f32[1024,640]{1,0:T(8,128)}, ...) | async-done | bytes 14417936 | tf_op jit(solution)/shard_map/psum | solution.py:316
  1464.6 78.7 %all-reduce.20.cloned.1.call-done = (f32[1024]{0:T(1024)}, f32[256,16]{0,1:T(8,128)}, f32[256,16]{0,1:T(8,128)}, f32[256,16]{0,1:T(8,128)}, f32[256,16]{0,1:T(8,...) async-done(((f32[1024]{0:T(1024)}, f32[256,16]{0,1:T(8,128)}, ...) | async-done | bytes 110608 | tf_op jit(solution)/shard_map/psum | solution.py:316
  (932 shorter events, 657.0 us)
Async XLA Ops:
  7.2 451.2 %copy-start = (bf16[640,1024]{1,0:T(8,128)(2,1)S(1)}, bf16[640,1024]{1,0:T(8,128)(2,1)}, u32[]{:S(2)}) copy-start(bf16[640,1024]{1,0:T(8,128)(2,1)} %param.63) | copy-start | bytes 3932164
  7.2 27.7 %all-gather.5.cloned.1.call-start = ((), (), s32[]{:S(2)}) async-start(), calls=%async_computation.4 | async-start | bytes 2621440 | tf_op jit(solution)/shard_map/all_gather | solution.py:125
  8.0 305.5 %all-reduce.16.cloned.1.call-start = ((), (), s32[]{:S(2)}) async-start(), calls=%async_computation.5 | async-start | bytes 2097152 | tf_op jit(solution)/shard_map/psum | solution.py:176
  8.8 6.9 copy-start.51
  8.8 6.9 copy-start.61
  25.1 12.1 copy-start.72
  277.3 61.7 %all-gather.7.cloned.1.call-start = ((), (), s32[]{:S(2)}) async-start(), calls=%async_computation.6 | async-start | bytes 2621440 | tf_op jit(solution)/shard_map/all_gather | solution.py:175
  278.0 156.2 %all-reduce.18.cloned.1.call-start = ((), (), s32[]{:S(2)}) async-start(), calls=%async_computation.7 | async-start | bytes 8388608 | tf_op jit(solution)/shard_map/psum | solution.py:200
  279.7 33.8 %copy-start.82 = (f32[256]{0:T(256)S(1)}, f32[256]{0:T(256)}, u32[]{:S(2)}) copy-start(f32[256]{0:T(256)} %param.54) | copy-start | bytes 3076
  279.7 33.8 %copy-start.83 = (f32[256]{0:T(256)S(1)}, f32[256]{0:T(256)}, u32[]{:S(2)}) copy-start(f32[256]{0:T(256)} %param.56) | copy-start | bytes 3076
  279.7 33.8 %copy-start.90 = (f32[256]{0:T(256)S(1)}, f32[256]{0:T(256)}, u32[]{:S(2)}) copy-start(f32[256]{0:T(256)} %param.55) | copy-start | bytes 3076
  348.5 109.8 %all-gather.9.cloned.1.call-start = ((), (), s32[]{:S(2)}) async-start(), calls=%async_computation.9 | async-start | bytes 2621440 | tf_op jit(solution)/shard_map/all_gather | solution.py:126
  349.1 88.6 %copy-start.65 = (f32[1024]{0:T(1024)S(1)}, f32[1024]{0:T(1024)}, u32[]{:S(2)}) copy-start(f32[1024]{0:T(1024)} %param.60) | copy-start | bytes 12292
  349.1 166.9 %reduce-scatter.7.cloned.1.call-start = ((), (), s32[]{:S(2)}) async-start(), calls=%async_computation.10 | async-start | bytes 5242880 | tf_op jit(solution)/shard_map/reduce_scatter | solution.py:220
  471.4 71.8 %all-gather.11.cloned.1.call-start = ((), (), s32[]{:S(2)}) async-start(), calls=%async_computation.11 | async-start | bytes 2621440 | tf_op jit(solution)/shard_map/all_gather | solution.py:228
  471.5 48.9 %copy-start.78 = (f32[256]{0:T(256)}, f32[256]{0:T(256)S(1)}, u32[]{:S(2)}) copy-start(f32[256]{0:T(256)S(1)} %dynamic-slice.23) | copy-start | bytes 3076
  518.1 31.3 %copy-start.80 = (f32[256]{0:T(256)}, f32[256]{0:T(256)S(1)}, u32[]{:S(2)}) copy-start(f32[256]{0:T(256)S(1)} %broadcast_multiply_fusion.5) | copy-start | bytes 3076
  520.4 104.1 %reduce-scatter.9.cloned.1.call-start = ((), (), s32[]{:S(2)}) async-start(), calls=%async_computation.12 | async-start | bytes 5242880 | tf_op jit(solution)/shard_map/reduce_scatter | solution.py:267
  543.2 7.2 copy-start.95
  553.7 429.5 %reduce-scatter.5.cloned.1.call-start = ((), (), s32[]{:S(2)}) async-start(), calls=%async_computation.8 | async-start | bytes 5242880 | tf_op jit(solution)/shard_map/reduce_scatter | solution.py:212
  560.5 445.8 %reduce-scatter.11.cloned.1.call-start = ((), (), s32[]{:S(2)}) async-start(), calls=%async_computation.13 | async-start | bytes 5242880 | tf_op jit(solution)/shard_map/reduce_scatter | solution.py:279
  960.7 503.9 %all-reduce.22.cloned.1.call-start = ((), (), s32[]{:S(2)}) async-start(), calls=%async_computation.15 | async-start | bytes 28835840 | tf_op jit(solution)/shard_map/psum | solution.py:316
  982.8 560.5 %all-reduce.20.cloned.1.call-start = ((), (), s32[]{:S(2)}) async-start(), calls=%async_computation.14 | async-start | bytes 221184 | tf_op jit(solution)/shard_map/psum | solution.py:316
  994.7 7.0 copy-start.66
  994.7 7.0 copy-start.67
  994.7 7.0 copy-start.68
  994.7 11.6 copy-start.25
  999.8 22.2 %copy-start.21 = (f32[256,1024]{1,0:T(8,128)S(1)}, f32[256,1024]{1,0:T(8,128)}, u32[]{:S(2)}) copy-start(f32[256,1024]{1,0:T(8,128)} %reduce-scatter.7.cloned.1.call-done) | copy-start | bytes 3145732
  999.8 22.2 %copy-start.27 = (bf16[256,1024]{1,0:T(8,128)(2,1)S(1)}, bf16[256,1024]{1,0:T(8,128)(2,1)}, u32[]{:S(2)}) copy-start(bf16[256,1024]{1,0:T(8,128)(2,1)} %param.44) | copy-start | bytes 1572868
  999.8 22.2 %copy-start.79 = (f32[256]{0:T(256)S(1)}, f32[256]{0:T(256)}, u32[]{:S(2)}) copy-start(f32[256]{0:T(256)} %copy-done.78) | copy-start | bytes 3076
  999.8 22.2 %copy-start.81 = (f32[256]{0:T(256)S(1)}, f32[256]{0:T(256)}, u32[]{:S(2)}) copy-start(f32[256]{0:T(256)} %copy-done.80) | copy-start | bytes 3076
  1006.3 15.7 copy-start.29
  (115 other events, 342.3 us)
Sparse Core Ops, SparseCore 0:
  9.6 25.2 all-gather.4
  277.4 36.0 all-reduce.15
  315.7 23.2 all-gather.6
  348.7 85.4 all-reduce.17
  435.6 22.7 all-gather.8
  471.5 44.4 reduce-scatter.6
  520.6 22.5 all-gather.10
  553.8 55.3 reduce-scatter.8
  611.7 44.2 reduce-scatter.4
  960.8 45.4 reduce-scatter.10
  1013.3 451.2 all-reduce.21
  1471.9 71.3 all-reduce.19
where the time goes:
time: 1600 us; the launch traced here: 1580 us
  waiting for transfers between devices  736 us (46%)
  other arithmetic  440 us (28%)
  local copies, waits for them, and re-layouts  175 us (11%)
  matrix products  115 us (7%)
  blocking collectives  46 us (3%)
  loops' own time  43.5 us (3%)
    psum x2, waiting for transfers between devices, on_device(): lax.psum((gain_sums[0], grad_alpha, grad_delta, grad_theta, grad_beta, gr...  519 us
    add_any x32, other arithmetic, decay_filter(): lax.scan(jax.checkpoint(one_block), initial, (signal.reshape(blocks, span...  130 us
    psum x1, waiting for transfers between devices, on_device(): branch = lax.psum(plain(product, w_attout), 'tensor')  84.6 us
    squeeze x80, local copies, waits for them, and re-layouts, decay_filter(): lax.scan(jax.checkpoint(one_block), initial, (signal.reshape(blocks, span...  61.1 us
    dot_general x32, other arithmetic, one_block(): jnp.einsum('tsc,sc->tc', toeplitz * same_doc[:, :, None], column, precisi...  57 us
    reduce_scatter x1, waiting for transfers between devices, on_device(): lax.psum_scatter(cross(d_gate, w_gate) + cross(d_up, w_up), 'tensor', sca...  44.5 us
    dynamic_update_slice x48, other arithmetic, decay_filter(): lax.scan(jax.checkpoint(one_block), initial, (signal.reshape(blocks, span...  43.7 us
    another operation x2, loops' own time, decay_filter(): lax.scan(jax.checkpoint(one_block), initial, (signal.reshape(blocks, span...  43.5 us
  transfers between devices with their start and end apart: 12, of which 10 were waited for; matrix products, arithmetic and copies ran while one was open for 27% of the time, Pallas kernels for 1%

commit v1 on v0

v1 whole, which is shorter than its diff:
```python
import functools
import math
import types

import jax
import jax.numpy as jnp
from jax import lax
from jax.experimental import pallas as pl
from jax.experimental.pallas import tpu as pltpu
from jax.sharding import PartitionSpec as P

epsilon = 1e-05
masked_score = -1000000000.0
f32 = jnp.float32
bf16 = jnp.bfloat16
MESH = pl.DeviceIdType.MESH
LANES = 128
SUB = 8
SPAN = 64
MAX_DOC = 512
PACK_TAIL = 32
VMEM_BYTES = 60 * 2**20


def plain(left, right):
    return jnp.dot(left, right, preferred_element_type=f32)


def cross(left, right):
    return lax.dot_general(
        left, right, (((1,), (1,)), ((), ())), preferred_element_type=f32
    )


def inner(left, right):
    return lax.dot_general(
        left, right, (((0,), (0,)), ((), ())), preferred_element_type=f32
    )


def sigmoid(value):
    return 1.0 / (1.0 + jnp.exp(-value))


def at(index, size):
    return pl.ds(pl.multiple_of(index * size, size), size)


class Stage:
    def __init__(self, ins, outs, scratch, refs):
        self.pending = {}
        self.flushed = []
        count = len(ins)
        self.hbm_in = dict(zip(ins, refs[:count]))
        self.hbm_out = dict(zip(outs, refs[count : count + len(outs)]))
        rest = refs[count + len(outs) :]
        names = list(ins) + list(outs) + list(scratch)
        self.refs = dict(zip(names, rest[: len(names)]))
        self.load_sem, self.flush_sem, self.send_sem, self.recv_sem = rest[len(names) :]
        self.order = {name: k for k, name in enumerate(ins)}
        self.out_order = {name: k for k, name in enumerate(outs)}
        self.used = 0
        self.names = {id(ref): name for name, ref in self.refs.items()}

    def __getitem__(self, name):
        return self.refs[name]

    def __getattr__(self, name):
        return self.refs[name]

    def load(self, *refs):
        for name in [self.names[id(ref)] for ref in refs]:
            copy = pltpu.make_async_copy(
                self.hbm_in[name], self.refs[name], self.load_sem.at[self.order[name]]
            )
            copy.start()
            self.pending[name] = copy

    def need(self, *refs):
        for name in [self.names[id(ref)] for ref in refs]:
            copy = self.pending.pop(name, None)
            if copy is not None:
                copy.wait()

    def flush(self, *refs):
        for name in [self.names[id(ref)] for ref in refs]:
            copy = pltpu.make_async_copy(
                self.refs[name], self.hbm_out[name], self.flush_sem.at[self.out_order[name]]
            )
            copy.start()
            self.flushed.append(copy)

    def close(self):
        for copy in self.flushed:
            copy.wait()

    def sems(self, count):
        first = self.used
        self.used += count
        return first

    def remote(self, source, target_ref, index, device):
        return pltpu.make_async_remote_copy(
            src_ref=source,
            dst_ref=target_ref,
            send_sem=self.send_sem.at[index],
            recv_sem=self.recv_sem.at[index],
            device_id=device,
            device_id_type=MESH,
        )


def run_stage(body, ins, outs, scratch, sems, collective):
    ins = vars(ins)

    def kernel(*refs):
        body(Stage(list(ins), list(outs), list(scratch), refs))

    buffers = [pltpu.VMEM(array.shape, array.dtype) for array in ins.values()]
    buffers += [pltpu.VMEM(shape, kind) for shape, kind in outs.values()]
    buffers += [pltpu.VMEM(shape, kind) for shape, kind in scratch.values()]
    results = pl.pallas_call(
        kernel,
        out_shape=tuple(jax.ShapeDtypeStruct(shape, kind) for shape, kind in outs.values()),
        in_specs=[pl.BlockSpec(memory_space=pl.ANY)] * len(ins),
        out_specs=tuple(pl.BlockSpec(memory_space=pl.ANY) for _ in outs),
        scratch_shapes=buffers
        + [
            pltpu.SemaphoreType.DMA((len(ins),)),
            pltpu.SemaphoreType.DMA((len(outs),)),
            pltpu.SemaphoreType.DMA((sems,)),
            pltpu.SemaphoreType.DMA((sems,)),
        ],
        compiler_params=pltpu.CompilerParams(
            collective_id=collective, has_side_effects=True, vmem_limit_bytes=VMEM_BYTES
        ),
    )(*ins.values())
    return types.SimpleNamespace(**dict(zip(outs, results)))


class Group:
    def __init__(self):
        self.me = lax.axis_index("tensor")
        chip = self.me // 2
        core = self.me % 2
        self.sib = chip * 2 + (1 - core)
        self.opp = (1 - chip) * 2 + core
        self.diag = (1 - chip) * 2 + (1 - core)

    def greet(self):
        barrier = pltpu.get_barrier_semaphore()
        for device in (self.sib, self.opp, self.diag):
            pl.semaphore_signal(barrier, inc=1, device_id={"tensor": device}, device_id_type=MESH)
        pl.semaphore_wait(barrier, 3)


class Gather:
    def __init__(self, stage, group, source, place, pieces):
        self.g = group
        self.pieces = pieces
        base = stage.sems(3 * pieces)
        opp = {"tensor": group.opp}
        sib = {"tensor": group.sib}
        self.to_opp = [
            stage.remote(source(s), place(group.me, s), base + s, opp) for s in range(pieces)
        ]
        self.to_sib = [
            stage.remote(source(s), place(group.me, s), base + pieces + s, sib)
            for s in range(pieces)
        ]
        self.passed = [
            stage.remote(place(group.opp, s), place(group.opp, s), base + 2 * pieces + s, sib)
            for s in range(pieces)
        ]

    def send(self, s):
        self.to_opp[s].start()
        self.to_sib[s].start()

    def forward(self, s):
        self.to_opp[s].wait_recv()
        self.passed[s].start()

    def near(self):
        for s in range(self.pieces):
            self.to_sib[s].wait_recv()

    def far(self):
        for s in range(self.pieces):
            self.passed[s].wait_recv()

    def close(self):
        for copy in self.to_opp + self.to_sib + self.passed:
            copy.wait_send()


class Scatter:
    def __init__(self, stage, group, name, pieces, order=None):
        self.order = list(order or range(pieces))
        self.out_diag = stage[name + "_od"]
        self.out_sib = stage[name + "_os"]
        self.out_opp = stage[name + "_oo"]
        self.in_opp = stage[name + "_io"]
        self.in_own = stage[name + "_iw"]
        self.in_far = stage[name + "_if"]
        self.rows = self.out_diag.shape[0] // pieces
        base = stage.sems(3 * pieces)

        def copies(source, target, first, device):
            return [
                stage.remote(
                    source.at[self.part(s)], target.at[self.part(s)], first + s, {"tensor": device}
                )
                for s in range(pieces)
            ]

        self.first = copies(self.out_diag, self.in_opp, base, group.sib)
        self.second = copies(self.out_sib, self.in_own, base + pieces, group.sib)
        self.across = copies(self.out_opp, self.in_far, base + 2 * pieces, group.opp)

    def part(self, s):
        return pl.ds(s * self.rows, self.rows)

    def put_diag(self, value):
        for s in self.order:
            self.out_diag[self.part(s), :] = value(s).astype(bf16)
            self.first[s].start()

    def put_opp(self, value):
        for s in self.order:
            mine = value(s)
            self.first[s].wait_recv()
            total = mine + self.in_opp[self.part(s), :].astype(f32)
            self.out_opp[self.part(s), :] = total.astype(bf16)
            self.across[s].start()

    def put_sib(self, value):
        for s in self.order:
            self.out_sib[self.part(s), :] = value(s).astype(bf16)
            self.second[s].start()

    def take(self, s, own):
        self.second[s].wait_recv()
        near = own + self.in_own[self.part(s), :].astype(f32)
        self.across[s].wait_recv()
        return near + self.in_far[self.part(s), :].astype(f32)

    def close(self):
        for copy in self.first + self.second + self.across:
            copy.wait_send()


def pieces_of(value, count):
    rows = value.shape[0] // count
    return lambda s: value[s * rows : (s + 1) * rows]


def scatter_buffers(name, rows, width):
    return {
        name + tail: ((rows, width), bf16) for tail in ("_od", "_os", "_oo", "_io", "_iw", "_if")
    }


def ring_seats(count):
    index = lax.axis_index("dp")
    place = jnp.where(index % 2 == 0, index // 2, count - 1 - index // 2)

    def seat(p):
        p = lax.rem(p + 2 * count, count)
        return jnp.where(2 * p < count, 2 * p, 2 * (count - 1 - p) + 1)

    return place, seat


def ring_rows(shape, kind, count):
    tile = 16 if kind == bf16 else SUB
    if shape[0] % (2 * count * tile) == 0:
        return shape[0] // (2 * count), shape[1]
    if shape[0] % (count * tile) == 0 and shape[1] % (2 * LANES) == 0:
        return shape[0] // count, shape[1] // 2
    return None


class Ring:
    def __init__(self, m, count, items):
        self.m = m
        self.count = count
        self.items = items
        self.place, self.seat = ring_seats(count)
        self.steps = 2 * (count - 1)
        self.base = m.sems(len(items) * 2 * self.steps)
        self.sent = []

    def greet(self, barrier):
        for step in (-1, 1):
            device = self.seat(self.place + step)
            pl.semaphore_signal(barrier, inc=1, device_id={"dp": device}, device_id_type=MESH)

    def view(self, ref, chunk, way):
        shape = ref.shape
        rows, columns = ring_rows(shape, ref.dtype, self.count)
        chunk = lax.rem(chunk + 2 * self.count, self.count)
        if columns == shape[1]:
            return ref.at[pl.ds(pl.multiple_of((2 * chunk + way) * rows, rows), rows), :]
        return ref.at[
            pl.ds(pl.multiple_of(chunk * rows, rows), rows), pl.ds(way * columns, columns)
        ]

    def copy(self, item, way, step):
        own, box, total = self.items[item]
        sign = 1 - 2 * way
        last = self.count - 1
        index = self.base + (2 * item + way) * self.steps + step
        if step < last:
            source = self.view(own, self.place, way) if step == 0 else box.at[way, step - 1]
            target = box.at[way, step]
        else:
            source = self.view(total, self.place + sign - sign * (step - last), way)
            target = source
        return self.m.remote(source, target, index, {"dp": self.seat(self.place + sign)})

    def start(self, item, way, step):
        copy = self.copy(item, way, step)
        copy.start()
        self.sent.append(copy)

    def begin(self):
        for item in range(len(self.items)):
            for way in range(2):
                self.start(item, way, 0)

    def tick(self, step):
        last = self.count - 1
        for item, (own, box, total) in enumerate(self.items):
            for way in range(2):
                sign = 1 - 2 * way
                self.copy(item, way, step).wait_recv()
                if step < last:
                    chunk = self.place - sign * (step + 1)
                    value = box[way, step].astype(f32) + self.view(own, chunk, way)[...].astype(f32)
                    if step < last - 1:
                        box[way, step] = value.astype(box.dtype)
                    else:
                        self.view(total, chunk, way)[...] = value.astype(total.dtype)
                if step + 1 < self.steps:
                    self.start(item, way, step + 1)

    def close(self):
        for copy in self.sent:
            copy.wait_send()


def ring_box(shape, kind, count):
    rows, columns = ring_rows(shape, kind, count)
    return ((2, count - 1, rows, columns), kind)


def run_ring(arrays, count, collective):
    names = list(arrays)
    outs = {name + "t": (array.shape, array.dtype) for name, array in arrays.items()}
    scratch = {name + "b": ring_box(a.shape, a.dtype, count) for name, a in arrays.items()}

    def body(m):
        refs = [(m[name], m[name + "b"], m[name + "t"]) for name in names]
        m.load(*[own for own, _, _ in refs])
        ring = Ring(m, count, refs)
        barrier = pltpu.get_barrier_semaphore()
        ring.greet(barrier)
        pl.semaphore_wait(barrier, 2)
        m.need(*[own for own, _, _ in refs])
        ring.begin()
        for step in range(ring.steps):
            ring.tick(step)
        for _, _, total in refs:
            m.flush(total)
        ring.close()
        m.close()

    sems = len(names) * 4 * (count - 1)
    done = run_stage(
        body, types.SimpleNamespace(**arrays), outs, scratch, sems, collective
    )
    return [getattr(done, name + "t") for name in names]


def sum_over_dp(arrays, collective):
    count = lax.axis_size("dp")
    if count > 1 and count % 2 == 0 and all(
        ring_rows(a.shape, a.dtype, count) for a in arrays.values()
    ):
        return run_ring(arrays, count, collective)
    return lax.psum([array.astype(f32) for array in arrays.values()], "dp")


def tables_of(ema_alpha, ema_delta, ema_theta, ema_beta, eta_real, eta_imag):
    magnitude = 1.0 - ema_alpha * ema_delta
    cosine, sine = jnp.cos(ema_theta), jnp.sin(ema_theta)
    scaled = ema_alpha * ema_beta
    stacked = jnp.stack(
        [
            magnitude * cosine,
            magnitude * sine,
            scaled * eta_real,
            scaled * eta_imag,
            cosine,
            sine,
            ema_alpha,
            ema_delta,
            ema_beta,
            eta_real,
            eta_imag,
        ]
    )
    return jnp.swapaxes(stacked, 1, 2)


def groups(array):
    halves = array.shape[0] // SUB
    sides = array.shape[1] // LANES
    return [
        array[SUB * s : SUB * s + SUB, LANES * l : LANES * l + LANES]
        for s in range(halves)
        for l in range(sides)
    ]


def spread_row(ref, index):
    return jnp.broadcast_to(ref[index], (SUB, LANES))


def advance(state, coefs, keep, signals, sides):
    root_real, root_imag = coefs
    half = len(state) // 2
    kept = [value * keep for value in state]
    fresh = [None] * len(state)
    for g in range(half):
        a_real, a_imag = kept[g], kept[half + g]
        fresh[g] = (root_real[g] * a_real - root_imag[g] * a_imag) + signals[g % sides]
        fresh[half + g] = root_real[g] * a_imag + root_imag[g] * a_real
    return kept, fresh


def filter_forward(m, first, count, state):
    sides = m.xl.shape[0]
    tables = m.tab
    root_real, root_imag = groups(tables[0]), groups(tables[1])
    out_real, out_imag = groups(tables[2]), groups(tables[3])
    half = len(root_real)
    unroll = 16

    def chunk(ch, state):
        for g in range(2 * half):
            m.st[ch, g] = state[g]

        def steps(i, state):
            state = list(state)
            for j in range(unroll):
                t = ch * SPAN + i * unroll + j
                keep = spread_row(m.kf, (pl.ds(t, 1), slice(None)))
                signals = [
                    spread_row(m.xl, (l, pl.ds(t, 1), slice(None))) for l in range(sides)
                ]
                _, state = advance(state, (root_real, root_imag), keep, signals, sides)
                for l in range(sides):
                    total = None
                    for g in range(l, half, sides):
                        term = out_real[g] * state[g] - out_imag[g] * state[half + g]
                        total = term if total is None else total + term
                    m.part[l, pl.ds(pl.multiple_of((i * unroll + j) * SUB, SUB), SUB), :] = total
            return tuple(state)

        state = lax.fori_loop(0, SPAN // unroll, steps, state)
        rows = at(ch, SPAN)
        for l in range(sides):
            lanes = slice(LANES * l, LANES * l + LANES)
            value = m.om[:, lanes] * m.xl[l, rows, :]
            for s in range(SUB):
                value = value + m.part[l, pl.ds(s, SPAN, stride=SUB), :]
            gate = sigmoid(value)
            m.mxl[rows, lanes] = (value * gate).astype(bf16)
            m.se[rows, lanes] = gate * (1.0 + value * (1.0 - gate))
        return state

    return lax.fori_loop(first, first + count, chunk, state)


def window_mask(m, first_row, rows, first_key, keys):
    same = m.segc[pl.ds(pl.multiple_of(first_row, LANES), rows), :] == m.segr[
        :, pl.ds(pl.multiple_of(first_key, LANES), keys)
    ]
    row = first_row + lax.broadcasted_iota(jnp.int32, (rows, keys), 0)
    key = first_key + lax.broadcasted_iota(jnp.int32, (rows, keys), 1)
    return same & (row >= key)


def window_of(index, block, length):
    back = -(-MAX_DOC // block)
    keys = min((back + 1) * block, length)
    first = jnp.maximum(index - back, 0) * block
    first = jnp.minimum(first, length - keys)
    return pl.multiple_of(first, LANES), keys


def body_a(m):
    g = Group()
    length, width = m.xt.shape
    block = m.tok.shape[0]
    blocks = length // block
    channels = m.mxl.shape[1]
    sides = channels // LANES
    m.load(m.tok, m.wsh, m.kf, m.segc, m.segr, m.gain, m.tab, m.om, m.wv, m.cot, m.wag)
    m.load(m.qg, m.qb, m.kg, m.wo, m.rg)
    g.greet()

    own = at(g.me, block)
    half = block // 2
    tokens = Gather(
        m, g,
        lambda s: m.tok.at[pl.ds(s * half, half), :],
        lambda j, s: m.xt.at[pl.ds(pl.multiple_of(j * block + s * half, half), half), :],
        2,
    )
    shared = Gather(m, g, lambda s: m.wsh, lambda j, s: m.wsf.at[at(j, channels), :], 1)
    pieces = 4
    rows_piece = length // pieces
    mixed = Gather(
        m, g,
        lambda s: m.mxl.at[pl.ds(s * rows_piece, rows_piece), :],
        lambda j, s: m.mx.at[pl.ds(s * rows_piece, rows_piece), at(j, channels)],
        pieces,
    )
    cots = Gather(
        m, g,
        lambda s: m.cot.at[pl.ds(s * half, half), :],
        lambda j, s: m.cotf.at[pl.ds(pl.multiple_of(j * block + s * half, half), half), :],
        2,
    )
    normed = Gather(
        m, g,
        lambda s: m.yno.at[pl.ds(s * half, half), :],
        lambda j, s: m.yn.at[pl.ds(pl.multiple_of(j * block + s * half, half), half), :],
        2,
    )
    branch = Scatter(m, g, "br", 2)

    m.need(m.tok, m.wsh)
    tokens.send(0)
    tokens.send(1)
    shared.send(0)
    m.xt[own, :] = m.tok[...]
    m.wsf[at(g.me, channels), :] = m.wsh[...]
    m.need(m.kf, m.segc, m.segr, m.gain, m.tab, m.om)

    lane = lax.broadcasted_iota(jnp.int32, (SPAN, LANES), 1)

    def sums(j):
        def part(i, _):
            rows = pl.ds(pl.multiple_of(j * block + i * SPAN, SPAN), SPAN)
            one = jnp.zeros((SPAN, LANES), f32)
            two = jnp.zeros((SPAN, LANES), f32)
            for l in range(width // LANES):
                x = m.xt[rows, LANES * l : LANES * l + LANES].astype(f32)
                one = one + x
                two = two + x * x
            picked = jnp.where(lane == 6, 1.0, 0.0)
            for k, total in ((0, one), (3, two)):
                rest = jnp.sum(total, axis=1, keepdims=True)
                for n in range(3):
                    top = rest.astype(bf16).astype(f32)
                    picked = jnp.where(lane == k + n, top, picked)
                    rest = rest - top
            m.sums[rows, :] = picked.astype(bf16)
            return 0

        lax.fori_loop(0, block // SPAN, part, 0)

    sums(g.me)
    tokens.near()
    sums(g.sib)
    tokens.forward(0)
    tokens.forward(1)
    shared.forward(0)
    sums(g.opp)
    tokens.far()
    sums(g.diag)

    lane_wide = lax.broadcasted_iota(jnp.int32, (block, LANES), 1)

    def statistics(i, _):
        first, keys = window_of(i, block, length)
        seen = window_mask(m, i * block, block, first, keys).astype(bf16)
        got = plain(seen, m.sums[pl.ds(first, keys), :])
        pick = lambda low, high: jnp.sum(
            jnp.where((lane_wide >= low) & (lane_wide < high), got, 0.0), axis=1, keepdims=True
        )
        total = pick(6, 7) * width
        mean = pick(0, 3) / total
        var = pick(3, 6) / total - mean * mean
        rows = at(i, block)
        m.mean[rows, :] = jnp.broadcast_to(mean, (block, LANES))
        m.rstd[rows, :] = jnp.broadcast_to(lax.rsqrt(var + epsilon), (block, LANES))
        m.total[rows, :] = jnp.broadcast_to(total, (block, LANES))
        return 0

    lax.fori_loop(0, blocks, statistics, 0)

    def normalise(i, _):
        rows = at(i, SPAN)
        mean, rstd = m.mean[rows, :], m.rstd[rows, :]
        for l in range(width // LANES):
            lanes = slice(LANES * l, LANES * l + LANES)
            x = m.xt[rows, lanes].astype(f32)
            m.xn[rows, lanes] = ((x - mean) * rstd * m.gain[:, lanes]).astype(bf16)
        for l in range(sides):
            lanes = pl.ds(pl.multiple_of(g.me * channels + LANES * l, LANES), LANES)
            x = m.xt[rows, lanes].astype(f32)
            m.xl[l, rows, :] = (x - mean) * rstd * m.gain[:, lanes]
        return 0

    lax.fori_loop(0, length // SPAN, normalise, 0)
    own_stat = pl.ds(pl.multiple_of(g.me * block, block), block)
    m.so[0] = m.mean[own_stat, :]
    m.so[1] = m.rstd[own_stat, :]
    m.so[2] = m.total[own_stat, :]
    m.flush(m.xn, m.xl, m.so)

    zero = jnp.zeros((SUB, LANES), f32)
    state = tuple(zero for _ in range(m.st.shape[1]))
    per = length // SPAN // pieces
    for p in range(pieces):
        state = filter_forward(m, p * per, per, state)
        mixed.send(p)
        if p >= 2:
            mixed.forward(p - 2)
    m.need(m.cot)
    cots.send(0)
    cots.send(1)
    m.flush(m.se, m.st)
    for i in range(pieces):
        m.mx[pl.ds(i * rows_piece, rows_piece), at(g.me, channels)] = m.mxl[
            pl.ds(i * rows_piece, rows_piece), :
        ]
    m.cotf[own, :] = m.cot[...]
    m.need(m.wv)

    def values(i, _):
        rows = at(i, block)
        pre = plain(m.xn[rows, :], m.wv[...])
        gate = sigmoid(pre)
        m.v[rows, :] = (pre * gate).astype(bf16)
        m.sv[rows, :] = (gate * (1.0 + pre * (1.0 - gate))).astype(bf16)
        return 0

    lax.fori_loop(0, blocks, values, 0)
    m.flush(m.v, m.sv)
    for p in range(max(pieces - 2, 0), pieces):
        mixed.forward(p)
    shared.near()
    shared.far()
    mixed.near()
    mixed.far()
    m.need(m.qg, m.qb, m.kg, m.wag, m.wo, m.rg)

    def project(i, _):
        rows = at(i, block)
        z = plain(m.mx[rows, :], m.wsf[...])
        m.z[rows, :] = z
        m.q[rows, :] = (z * m.qg[...] + m.qb[...]).astype(bf16)
        m.k[rows, :] = (z * m.kg[...]).astype(bf16)
        return 0

    lax.fori_loop(0, blocks, project, 0)
    m.flush(m.mx, m.wsf, m.z, m.q, m.k)
    scale = 1.0 / math.sqrt(m.q.shape[1])

    def attend(i):
        rows = at(i, block)
        first, keys = window_of(i, block, length)
        window = pl.ds(first, keys)
        scores = cross(m.q[rows, :], m.k[window, :]) * scale
        scores = jnp.where(window_mask(m, i * block, block, first, keys), scores, masked_score)
        expo = jnp.exp(scores - jnp.max(scores, axis=1, keepdims=True))
        prob = (expo / jnp.sum(expo, axis=1, keepdims=True)).astype(bf16)
        m.p[i] = prob
        attended = plain(prob, m.v[window, :])
        pre = plain(m.mx[rows, :], m.wag[...])
        gate = sigmoid(pre)
        swish = pre * gate
        m.r[rows, :] = swish.astype(bf16)
        m.os[rows, :] = (attended * (gate * (1.0 + pre * (1.0 - gate)))).astype(bf16)
        m.w[rows, :] = (attended * swish).astype(bf16)
        return plain(m.w[rows, :], m.wo[...])

    branch.put_diag(pieces_of(attend(g.diag), 2))
    cots.forward(0)
    cots.forward(1)
    branch.put_opp(pieces_of(attend(g.opp), 2))
    branch.put_sib(pieces_of(attend(g.sib), 2))
    m.bp[...] = attend(g.me)
    m.flush(m.p, m.r, m.os, m.w)
    for s in range(2):
        piece = pl.ds(s * half, half)
        y = branch.take(s, m.bp[piece, :]) + m.tok[piece, :].astype(f32)
        m.y[piece, :] = y
        rms = lax.rsqrt(jnp.mean(y * y, axis=1, keepdims=True) + epsilon)
        m.rs[piece, :] = jnp.broadcast_to(rms, (half, LANES))
        m.yno[piece, :] = (y * rms * m.rg[...]).astype(bf16)
        normed.send(s)
    m.yn[own, :] = m.yno[...]
    m.flush(m.y, m.rs)
    cots.near()
    cots.far()
    m.flush(m.cotf)
    normed.forward(0)
    normed.forward(1)
    normed.near()
    normed.far()
    m.flush(m.yn)
    for moved in (tokens, shared, mixed, cots, normed, branch):
        moved.close()
    m.close()


def run_a(arrays, sizes):
    length, width, block, channels, shared, values = sizes
    blocks = length // block
    keys = min((-(-MAX_DOC // block) + 1) * block, length)
    sides = channels // LANES
    states = 2 * sides * (arrays.tab.shape[1] // SUB)
    outs = dict(
        xn=((length, width), bf16),
        xl=((sides, length, LANES), f32),
        so=((3, block, LANES), f32),
        se=((length, channels), f32),
        st=((length // SPAN, states, SUB, LANES), f32),
        mx=((length, width), bf16),
        v=((length, values), bf16),
        sv=((length, values), bf16),
        z=((length, shared), f32),
        q=((length, shared), bf16),
        k=((length, shared), bf16),
        wsf=((width, shared), bf16),
        p=((blocks, block, keys), bf16),
        r=((length, values), bf16),
        os=((length, values), bf16),
        w=((length, values), bf16),
        y=((block, width), f32),
        rs=((block, LANES), f32),
        yn=((length, width), bf16),
        cotf=((length, width), bf16),
    )
    scratch = dict(
        xt=((length, width), bf16),
        sums=((length, LANES), bf16),
        mean=((length, LANES), f32),
        rstd=((length, LANES), f32),
        total=((length, LANES), f32),
        part=((sides, SPAN * SUB, LANES), f32),
        mxl=((length, channels), bf16),
        bp=((block, width), f32),
        yno=((block, width), bf16),
        **scatter_buffers("br", block, width),
    )
    return run_stage(body_a, arrays, outs, scratch, 64, 1)


def transposed_product(m, left, right, out, step):
    def part(i, _):
        columns = at(i, step)
        out[columns, :] = inner(left[:, columns], right[...]).astype(bf16)
        return 0

    lax.fori_loop(0, left.shape[1] // step, part, 0)
    m.flush(out)


def body_b(m):
    g = Group()
    length, width = m.yn.shape
    block = m.y.shape[0]
    half = block // 2
    m.load(m.yn, m.wg, m.wu, m.wd, m.cotf, m.y, m.rs, m.cot, m.rg)
    g.greet()
    grads = Scatter(m, g, "dy", 2)
    fed = Scatter(m, g, "ff", 2)
    back = Gather(
        m, g,
        lambda s: m.dyo.at[pl.ds(s * half, half), :],
        lambda j, s: m.dyf.at[pl.ds(pl.multiple_of(j * block + s * half, half), half), :],
        2,
    )
    m.need(m.yn, m.wg, m.wu, m.wd, m.cotf)

    def feed(j):
        rows = at(j, block)
        low = m.yn[rows, :]
        gate = plain(low, m.wg[...])
        up = plain(low, m.wu[...])
        d_act = cross(m.cotf[rows, :], m.wd[...])
        sig = sigmoid(gate)
        swish = gate * sig
        m.act[rows, :] = (swish * up).astype(bf16)
        m.dg[rows, :] = (d_act * up * (sig * (1.0 + gate * (1.0 - sig)))).astype(bf16)
        m.du[rows, :] = (d_act * swish).astype(bf16)
        return cross(m.dg[rows, :], m.wg[...]) + cross(m.du[rows, :], m.wu[...])

    grads.put_diag(pieces_of(feed(g.diag), 2))
    grads.put_opp(pieces_of(feed(g.opp), 2))
    grads.put_sib(pieces_of(feed(g.sib), 2))
    m.bp[...] = feed(g.me)
    transposed_product(m, m.act, m.cotf, m.gd, LANES)
    m.need(m.y, m.rs, m.cot, m.rg)
    gain_sum = jnp.zeros((1, width), f32)
    for s in range(2):
        piece = pl.ds(s * half, half)
        d_yn = grads.take(s, m.bp[piece, :])
        rms = m.rs[piece, :][:, :1]
        hat = m.y[piece, :] * rms
        gain_sum = gain_sum + jnp.sum(d_yn * hat, axis=0, keepdims=True)
        d_hat = d_yn * m.rg[...]
        pull = d_hat - hat * jnp.mean(d_hat * hat, axis=1, keepdims=True)
        dy = m.cot[piece, :].astype(f32) + rms * pull
        m.dy[piece, :] = dy
        m.dyo[piece, :] = dy.astype(bf16)
        back.send(s)
    m.gr[...] = gain_sum
    m.dyf[at(g.me, block), :] = m.dyo[...]
    m.flush(m.dy, m.gr)
    share = lambda j: plain(m.act[at(j, block), :], m.wd[...])
    fed.put_diag(pieces_of(share(g.diag), 2))
    fed.put_opp(pieces_of(share(g.opp), 2))
    fed.put_sib(pieces_of(share(g.sib), 2))
    m.bp[...] = share(g.me)
    transposed_product(m, m.yn, m.dg, m.gg, 2 * LANES)
    back.forward(0)
    back.forward(1)
    transposed_product(m, m.yn, m.du, m.gu, 2 * LANES)
    back.near()
    back.far()
    m.flush(m.dyf)
    for s in range(2):
        piece = pl.ds(s * half, half)
        m.out[piece, :] = (fed.take(s, m.bp[piece, :]) + m.y[piece, :]).astype(bf16)
    m.flush(m.out)
    for moved in (grads, fed, back):
        moved.close()
    m.close()


def run_b(arrays, sizes):
    length, width, block, units = sizes
    outs = dict(
        gd=((units, width), bf16),
        gg=((width, units), bf16),
        gu=((width, units), bf16),
        dy=((block, width), f32),
        gr=((1, width), f32),
        dyf=((length, width), bf16),
        out=((block, width), bf16),
    )
    scratch = dict(
        act=((length, units), bf16),
        dg=((length, units), bf16),
        du=((length, units), bf16),
        bp=((block, width), f32),
        dyo=((block, width), bf16),
        **scatter_buffers("dy", block, width),
        **scatter_buffers("ff", block, width),
    )
    return run_stage(body_b, arrays, outs, scratch, 32, 2)


def filter_backward(m, last, count, gamma):
    sides = m.xl.shape[0]
    tables = m.tab
    root_real, root_imag = groups(tables[0]), groups(tables[1])
    out_real, out_imag = groups(tables[2]), groups(tables[3])
    half = len(root_real)
    unroll = 16

    def chunk(step, gamma):
        ch = last - step

        def again(i, state):
            state = list(state)
            for j in range(unroll):
                local = i * unroll + j
                t = ch * SPAN + local
                keep = spread_row(m.kf, (pl.ds(t, 1), slice(None)))
                signals = [
                    spread_row(m.xl, (l, pl.ds(t, 1), slice(None))) for l in range(sides)
                ]
                kept, state = advance(state, (root_real, root_imag), keep, signals, sides)
                for g in range(2 * half):
                    m.kept[local, g] = kept[g]
            return tuple(state)

        lax.fori_loop(0, SPAN // unroll, again, tuple(m.st[ch, g] for g in range(2 * half)))

        def reverse(i, carry):
            gamma, sums = list(carry[: 2 * half]), list(carry[2 * half :])
            for j in range(unroll):
                local = SPAN - 1 - (i * unroll + j)
                t = ch * SPAN + local
                keep = spread_row(m.kf, (pl.ds(t + 1, 1), slice(None)))
                signals = [
                    spread_row(m.de, (l, pl.ds(t, 1), slice(None))) for l in range(sides)
                ]
                _, gamma = advance(gamma, (root_real, root_imag), keep, signals, sides)
                for l in range(sides):
                    total = None
                    for g in range(l, half, sides):
                        g_real, g_imag = gamma[g], gamma[half + g]
                        a_real, a_imag = m.kept[local, g], m.kept[local, half + g]
                        term = out_real[g] * g_real - out_imag[g] * g_imag
                        total = term if total is None else total + term
                        sums[g] = sums[g] + (g_real * a_real - g_imag * a_imag)
                        sums[half + g] = sums[half + g] + (g_real * a_imag + g_imag * a_real)
                        sums[2 * half + g] = sums[2 * half + g] + signals[l] * a_real
                        sums[3 * half + g] = sums[3 * half + g] + signals[l] * a_imag
                    m.part[l, pl.ds(pl.multiple_of(local * SUB, SUB), SUB), :] = total
            return tuple(gamma) + tuple(sums)

        start = tuple(gamma) + tuple(m.acc[g] for g in range(4 * half))
        done = lax.fori_loop(0, SPAN // unroll, reverse, start)
        for g in range(4 * half):
            m.acc[g] = done[2 * half + g]
        rows = at(ch, SPAN)
        for l in range(sides):
            lanes = slice(LANES * l, LANES * l + LANES)
            signal = m.de[l, rows, :]
            value = m.om[:, lanes] * signal
            for s in range(SUB):
                value = value + m.part[l, pl.ds(s, SPAN, stride=SUB), :]
            m.dxb[rows, lanes] = value.astype(bf16)
            m.go[:, lanes] = m.go[:, lanes] + jnp.sum(
                signal * m.xl[l, rows, :], axis=0, keepdims=True
            )
        return done[: 2 * half]

    return lax.fori_loop(0, count, chunk, gamma)


def filter_gradients(m):
    sides = m.xl.shape[0]
    half = m.acc.shape[0] // 4
    dims = m.tab.shape[1]
    for g in range(half):
        s, l = g // sides, g % sides
        rows = slice(SUB * s, SUB * s + SUB)
        lanes = slice(LANES * l, LANES * l + LANES)
        q_re, q_im, c_re, c_im, cosine, sine, alpha, delta, beta, e_re, e_im = (
            m.tab[k, rows, lanes] for k in range(11)
        )
        lag_re, lag_im, sum_re, sum_im = (m.acc[k * half + g] for k in range(4))
        f_re = q_re * sum_re - q_im * sum_im + m.go[:, lanes]
        f_im = q_re * sum_im + q_im * sum_re
        scaled = alpha * beta
        d_scaled = e_re * f_re - e_im * f_im
        w_re = c_re * lag_re - c_im * lag_im
        w_im = c_re * lag_im + c_im * lag_re
        d_mag = w_re * cosine - w_im * sine
        m.pk[0 * dims + SUB * s : 0 * dims + SUB * s + SUB, lanes] = beta * d_scaled - delta * d_mag
        m.pk[1 * dims + SUB * s : 1 * dims + SUB * s + SUB, lanes] = -alpha * d_mag
        m.pk[2 * dims + SUB * s : 2 * dims + SUB * s + SUB, lanes] = -(w_re * q_im + w_im * q_re)
        m.pk[3 * dims + SUB * s : 3 * dims + SUB * s + SUB, lanes] = alpha * d_scaled
        m.pk[4 * dims + SUB * s : 4 * dims + SUB * s + SUB, lanes] = scaled * f_re
        m.pk[5 * dims + SUB * s : 5 * dims + SUB * s + SUB, lanes] = -scaled * f_im


def body_c(m):
    g = Group()
    length, width = m.dyf.shape
    block = m.tok.shape[0]
    blocks = length // block
    half = block // 2
    channels = m.se.shape[1]
    shared = m.q.shape[1]
    sides = channels // LANES
    m.load(m.dyf, m.wo, m.r, m.os, m.v, m.p, m.k, m.q, m.z, m.qg, m.kg, m.sv, m.wsf, m.wag)
    m.load(m.wv, m.w, m.mx, m.xn, m.se, m.st, m.xl, m.kf, m.tab, m.om, m.tok, m.so, m.gain)
    m.load(m.dy, m.gr, m.segc, m.segr)
    g.greet()
    pieces = 4
    dm = Scatter(m, g, "dm", pieces, range(pieces - 1, -1, -1))
    xv = Scatter(m, g, "xv", 2)
    sh = Scatter(m, g, "sh", 1)
    others = (g.sib, g.opp, g.diag)
    base = m.sems(9)
    parts = [
        m.remote(m.dxb.at[at(dev, block), :], m.dxr.at[k], base + k, {"tensor": dev})
        for k, dev in enumerate(others)
    ]
    small = [
        m.remote(m.smo, m.sm.at[g.me], base + 3 + k, {"tensor": dev})
        for k, dev in enumerate(others)
    ]
    tails = [
        m.remote(m.aro, m.ar.at[:, at(g.me, block)], base + 6 + k, {"tensor": dev})
        for k, dev in enumerate(others)
    ]

    scale = 1.0 / math.sqrt(shared)
    m.dk[...] = jnp.zeros(m.dk.shape, f32)
    m.dv[...] = jnp.zeros(m.dv.shape, f32)
    m.need(m.dyf, m.wo, m.r, m.os, m.v, m.p, m.k, m.q)

    def attend(i, _):
        rows = at(i, block)
        first, keys = window_of(i, block, length)
        window = pl.ds(first, keys)
        d_w = cross(m.dyf[rows, :], m.wo[...])
        d_o = (d_w * m.r[rows, :].astype(f32)).astype(bf16)
        m.drp[rows, :] = (d_w * m.os[rows, :].astype(f32)).astype(bf16)
        prob_low = m.p[i]
        prob = prob_low.astype(f32)
        weighed = prob * cross(d_o, m.v[window, :])
        d_s = (weighed - prob * jnp.sum(weighed, axis=1, keepdims=True)) * scale
        d_s = d_s.astype(bf16)
        m.dq[rows, :] = plain(d_s, m.k[window, :])
        m.dk[window, :] = m.dk[window, :] + inner(d_s, m.q[rows, :])
        m.dv[window, :] = m.dv[window, :] + inner(prob_low, d_o)
        return 0

    lax.fori_loop(0, blocks, attend, 0)
    m.need(m.z, m.qg, m.kg, m.sv, m.wsf, m.wag)

    def affine(i, sums):
        rows = at(i, block)
        d_q, d_k, z = m.dq[rows, :], m.dk[rows, :], m.z[rows, :]
        m.dz[rows, :] = (d_q * m.qg[...] + d_k * m.kg[...]).astype(bf16)
        m.dvp[rows, :] = (m.dv[rows, :] * m.sv[rows, :].astype(f32)).astype(bf16)
        new = (d_q * z, d_q, d_k * z)
        return tuple(s + jnp.sum(n, axis=0, keepdims=True) for s, n in zip(sums, new))

    aff = lax.fori_loop(0, blocks, affine, tuple(jnp.zeros((1, shared), f32) for _ in range(3)))
    m.smo[...] = jnp.zeros(m.smo.shape, f32)
    for n in range(3):
        m.smo[2 + n : 3 + n, :shared] = aff[n]

    def mixing(j):
        def value(s):
            rows = pl.ds(s * (length // pieces), length // pieces)
            return cross(m.dz[rows, :], m.wsf[at(j, channels), :]) + cross(
                m.drp[rows, :], m.wag[at(j, channels), :]
            )

        return value

    dm.put_diag(mixing(g.diag))
    dm.put_opp(mixing(g.opp))
    dm.put_sib(mixing(g.sib))
    m.need(m.wv)
    spread = lambda j: pieces_of(cross(m.dvp[at(j, block), :], m.wv[...]), 2)
    xv.put_diag(spread(g.diag))
    xv.put_opp(spread(g.opp))
    xv.put_sib(spread(g.sib))
    m.dxn[...] = cross(m.dvp[at(g.me, block), :], m.wv[...])
    m.need(m.w, m.mx, m.xn)
    transposed_product(m, m.w, m.dyf, m.gao, 2 * LANES)
    transposed_product(m, m.mx, m.drp, m.gag, 2 * LANES)
    transposed_product(m, m.xn, m.dvp, m.gv, 2 * LANES)
    split = lambda j: (lambda s: inner(m.mx[:, at(j, channels)], m.dz[...]))
    sh.put_diag(split(g.diag))
    sh.put_opp(split(g.opp))
    sh.put_sib(split(g.sib))
    m.shp[...] = split(g.me)(0)
    m.need(m.se, m.st, m.xl, m.kf, m.tab, m.om)
    half_states = m.acc.shape[0] // 4
    m.acc[...] = jnp.zeros(m.acc.shape, f32)
    m.go[...] = jnp.zeros(m.go.shape, f32)
    gamma = tuple(jnp.zeros((SUB, LANES), f32) for _ in range(2 * half_states))
    per = length // SPAN // pieces
    own_mix = mixing(g.me)
    for s in range(pieces - 1, -1, -1):
        rows = pl.ds(s * (length // pieces), length // pieces)
        d_e = dm.take(s, own_mix(s)) * m.se[rows, :]
        for l in range(sides):
            m.de[l, rows, :] = d_e[:, LANES * l : LANES * l + LANES]
        gamma = filter_backward(m, (s + 1) * per - 1, per, gamma)
        for k, dev in enumerate(others):

            @pl.when(dev == s)
            def _():
                parts[k].start()

    filter_gradients(m)
    base_row = m.pk.shape[0] - PACK_TAIL
    m.pk[base_row:, :] = jnp.zeros((PACK_TAIL, channels), f32)
    m.pk[base_row : base_row + 1, :] = m.go[...]
    m.gs[...] = sh.take(0, m.shp[...]).astype(bf16)
    m.flush(m.gs)
    m.need(m.tok, m.so, m.gain, m.dy, m.gr, m.segc, m.segr)
    for s in range(2):
        piece = pl.ds(s * half, half)
        m.dxn[piece, :] = xv.take(s, m.dxn[piece, :])
    own_columns = at(g.me, channels)
    m.dxn[:, own_columns] = m.dxn[:, own_columns] + m.dxb[at(g.me, block), :].astype(f32)
    for k, dev in enumerate(others):
        parts[k].wait_recv()
        columns = at(dev, channels)
        m.dxn[:, columns] = m.dxn[:, columns] + m.dxr[k].astype(f32)
    gain_sum = jnp.zeros((1, width), f32)
    lane = lax.broadcasted_iota(jnp.int32, (half, LANES), 1)
    for s in range(2):
        piece = pl.ds(s * half, half)
        mean, rstd, total = (m.so[n, piece, :][:, :1] for n in range(3))
        centred = m.tok[piece, :].astype(f32) - mean
        d_xn = m.dxn[piece, :]
        gain_sum = gain_sum + jnp.sum(d_xn * (centred * rstd), axis=0, keepdims=True)
        d_hat = d_xn * m.gain[...]
        d_var = -0.5 * rstd * rstd * rstd * jnp.sum(d_hat * centred, axis=1, keepdims=True)
        one = (-rstd * jnp.sum(d_hat, axis=1, keepdims=True) - 2.0 * mean * d_var) / total
        two = d_var / total
        m.dxn[piece, :] = d_hat * rstd + m.dy[piece, :]
        m.aw[piece, :] = jnp.where(lane == 0, one, jnp.where(lane == 1, two, 0.0))
    m.smo[0:1, :] = gain_sum
    m.smo[1:2, :] = m.gr[...]
    turned = m.aw[...].T
    for n in range(2):
        rest = turned[n : n + 1, :]
        for k in range(3):
            top = rest.astype(bf16).astype(f32)
            m.art[3 * n + k : 3 * n + k + 1, :] = top
            rest = rest - top
    m.art[6:8, :] = jnp.zeros((2, block), f32)
    m.art[8:16, :] = jnp.zeros((8, block), f32)
    m.aro[...] = m.art[...].astype(bf16)
    for copy in tails + small:
        copy.start()
    m.ar[:, at(g.me, block)] = m.aro[...]
    m.sm[g.me] = m.smo[...]
    back = -(-MAX_DOC // block)
    keys = min((back + 1) * block, length)
    first_key = pl.multiple_of(jnp.minimum(g.me * block, length - keys), LANES)
    first_row = pl.multiple_of(g.me * block, LANES)
    same = m.segc[pl.ds(first_row, block), :] == m.segr[:, pl.ds(first_key, keys)]
    row = first_row + lax.broadcasted_iota(jnp.int32, (block, keys), 0)
    key = first_key + lax.broadcasted_iota(jnp.int32, (block, keys), 1)
    seen = (same & (row <= key)).astype(bf16)
    for copy in tails:
        copy.wait_recv()
    pulled = cross(seen, m.ar[:, pl.ds(first_key, keys)])
    b_one = pulled[:, 0:1] + pulled[:, 1:2] + pulled[:, 2:3]
    b_two = pulled[:, 3:4] + pulled[:, 4:5] + pulled[:, 5:6]
    for s in range(2):
        piece = pl.ds(s * half, half)
        rows = slice(s * half, (s + 1) * half)
        x = m.tok[piece, :].astype(f32)
        m.gt[piece, :] = (m.dxn[piece, :] + b_one[rows] + 2.0 * x * b_two[rows]).astype(bf16)
    m.flush(m.gt)
    for copy in small:
        copy.wait_recv()
    total = m.sm[0]
    for j in range(1, m.sm.shape[0]):
        total = total + m.sm[j]
    per = width // channels
    for n in range(2):
        for k in range(per):
            row = base_row + 1 + n * per + k
            m.pk[row : row + 1, :] = total[n : n + 1, k * channels : (k + 1) * channels]
    for n in range(3):
        row = base_row + 1 + 2 * per + n
        m.pk[row : row + 1, :shared] = total[2 + n : 3 + n, :shared]
    m.flush(m.pk)
    for moved in (dm, xv, sh):
        moved.close()
    for copy in parts + small + tails:
        copy.wait_send()
    m.close()


def run_c(arrays, sizes):
    length, width, block, channels, shared, values = sizes
    sides = channels // LANES
    half_states = sides * (arrays.tab.shape[1] // SUB)
    outs = dict(
        gao=((values, width), bf16),
        gag=((width, values), bf16),
        gv=((width, values), bf16),
        gs=((channels, shared), bf16),
        pk=((6 * arrays.tab.shape[1] + PACK_TAIL, channels), f32),
        gt=((block, width), bf16),
    )
    scratch = dict(
        dk=((length, shared), f32),
        dv=((length, values), f32),
        dq=((length, shared), f32),
        drp=((length, values), bf16),
        dz=((length, shared), bf16),
        dvp=((length, values), bf16),
        dxn=((block, width), f32),
        shp=((channels, shared), f32),
        go=((1, channels), f32),
        acc=((4 * half_states, SUB, LANES), f32),
        kept=((SPAN, 2 * half_states, SUB, LANES), f32),
        part=((sides, SPAN * SUB, LANES), f32),
        de=((sides, length, LANES), f32),
        dxb=((length, channels), bf16),
        dxr=((3, block, channels), bf16),
        aw=((block, LANES), f32),
        art=((16, block), f32),
        aro=((16, block), bf16),
        ar=((16, length), bf16),
        smo=((SUB, width), f32),
        sm=((length // block, SUB, width), f32),
        **scatter_buffers("dm", length, channels),
        **scatter_buffers("xv", block, width),
        **scatter_buffers("sh", channels, shared),
    )
    done = run_stage(body_c, arrays, outs, scratch, 48, 3)
    done.dims = arrays.tab.shape[1]
    return done


def finish(a, b, c, shared):
    sums = sum_over_dp(
        dict(gg=b.gg, gu=b.gu, gd=b.gd, gao=c.gao, gag=c.gag, gv=c.gv, gs=c.gs, pk=c.pk), 4
    )
    gg, gu, gd, gao, gag, gv, gs, pk = (value.astype(f32) for value in sums)
    dims = c.dims
    tables = [pk[dims * k : dims * k + dims].T for k in range(6)]
    top = 6 * dims
    width = gao.shape[1]
    per = width // pk.shape[1]
    norm = pk[top + 1 : top + 1 + per].reshape(width)
    rms = pk[top + 1 + per : top + 1 + 2 * per].reshape(width)
    aff = pk[top + 1 + 2 * per :, :shared]
    return (
        b.out, c.gt, norm, *tables, pk[top], gs, aff[0], aff[1], aff[2], gag, gv, gao,
        rms, gg, gu, gd,
    )


def on_device(
    tokens,
    segments,
    cotangent,
    timestep_norm_gain,
    ema_alpha,
    ema_delta,
    ema_theta,
    ema_beta,
    eta_real,
    eta_imag,
    ema_omega,
    w_shared,
    q_gain,
    q_bias,
    k_gain,
    w_attgate,
    w_value,
    w_attout,
    rms_gain,
    w_gate,
    w_up,
    w_down,
):
    block, width = tokens.shape
    length = segments.shape[1]
    channels, dims = ema_alpha.shape
    shared = w_shared.shape[1]
    values = w_value.shape[1]
    units = w_gate.shape[1]
    tab = tables_of(ema_alpha, ema_delta, ema_theta, ema_beta, eta_real, eta_imag)
    om = ema_omega[None]
    gain, rg = timestep_norm_gain[None], rms_gain[None]
    qg, qb, kg = q_gain[None], q_bias[None], k_gain[None]
    segc, segr = segments.reshape(length, 1), segments
    keep = (segments[0, 1:] == segments[0, :-1]).astype(f32)
    keep = jnp.concatenate([jnp.zeros((1,), f32), keep, jnp.zeros((SUB,), f32)])
    kf = jnp.broadcast_to(keep[:, None], (length + SUB, LANES))
    a = run_a(
        types.SimpleNamespace(
            tok=tokens, cot=cotangent, wsh=w_shared, segc=segc, segr=segr, kf=kf, gain=gain,
            tab=tab, om=om, qg=qg, qb=qb, kg=kg, wag=w_attgate, wv=w_value, wo=w_attout, rg=rg,
        ),
        (length, width, block, channels, shared, values),
    )
    b = run_b(
        types.SimpleNamespace(
            yn=a.yn, wg=w_gate, wu=w_up, wd=w_down, cotf=a.cotf, y=a.y, rs=a.rs,
            cot=cotangent, rg=rg,
        ),
        (length, width, block, units),
    )
    c = run_c(
        types.SimpleNamespace(
            dyf=b.dyf, wo=w_attout, r=a.r, os=a.os, v=a.v, p=a.p, k=a.k,
            q=a.q, z=a.z, qg=qg, kg=kg, sv=a.sv, wsf=a.wsf, wag=w_attgate,
            wv=w_value, w=a.w, mx=a.mx, xn=a.xn, se=a.se, st=a.st, xl=a.xl,
            kf=kf, tab=tab, om=om, tok=tokens, so=a.so, gain=gain, dy=b.dy, gr=b.gr,
            segc=segc, segr=segr,
        ),
        (length, width, block, channels, shared, values),
    )
    return finish(a, b, c, shared)


def solution(mesh):
    placed = (
        P(("dp", "tensor"), None),
        P("dp", None),
        P(("dp", "tensor"), None),
        P(),
        P("tensor", None),
        P("tensor", None),
        P("tensor", None),
        P("tensor", None),
        P("tensor", None),
        P("tensor", None),
        P("tensor"),
        P("tensor", None),
        P(),
        P(),
        P(),
        P(None, "tensor"),
        P(None, "tensor"),
        P("tensor", None),
        P(),
        P(None, "tensor"),
        P(None, "tensor"),
        P("tensor", None),
    )
    return jax.shard_map(
        on_device,
        mesh=mesh,
        in_specs=placed,
        out_specs=(
            P(("dp", "tensor"), None),
            P(("dp", "tensor"), None),
            P(),
            P("tensor", None),
            P("tensor", None),
            P("tensor", None),
            P("tensor", None),
            P("tensor", None),
            P("tensor", None),
            P("tensor"),
            P("tensor", None),
            P(),
            P(),
            P(),
            P(None, "tensor"),
            P(None, "tensor"),
            P("tensor", None),
            P(),
            P(None, "tensor"),
            P(None, "tensor"),
            P("tensor", None),
        ),
        check_vma=False,
    )
```

time: 1600 us -> 373 us (0.23)
  waiting for transfers between devices: 736 us -> 0 us
  other arithmetic: 440 us -> 16.6 us
  Pallas kernels: 8.71 us -> 337 us
  local copies, waits for them, and re-layouts: 175 us -> 14 us
  matrix products: 115 us -> 0 us
  blocking collectives: 46 us -> 0 us
  loops' own time: 43.5 us -> 0 us
    psum x4 -> x0, waiting for transfers between devices: 632 us -> none  [the longest x2 519 us: on_device(): lax.psum((gain_sums[0], grad_alpha, grad_delta, grad_theta, grad_beta, gr...]
    pallas_call x0 -> x4, Pallas kernels: none -> 337 us  [run_stage(): pl.pallas_call(kernel, out_shape=tuple((jax.ShapeDtypeStruct(shape, kind)...]
    add_any x52 -> x0, other arithmetic: 134 us -> none  [the longest x32 130 us: decay_filter(): lax.scan(jax.checkpoint(one_block), initial, (signal.reshape(blocks, span...]
    dot_general x36 -> x0, matrix products: 115 us -> none  [the longest x11 39 us: cross(): lax.dot_general(left, right, (((1,), (1,)), ((), ())), preferred_element_...]
    reduce_sum x45 -> x0, other arithmetic: 92.1 us -> none  [the longest x16 38.4 us: one_block(): entry_real * state_real[None] - entry_imag * state_imag[None]]
    dot_general x64 -> x0, other arithmetic: 70.1 us -> none  [the longest x32 57 us: one_block(): jnp.einsum('tsc,sc->tc', toeplitz * same_doc[:, :, None], column, precisi...]
    squeeze x81 -> x0, local copies, waits for them, and re-layouts: 61.8 us -> none  [the longest x80 61.1 us: decay_filter(): lax.scan(jax.checkpoint(one_block), initial, (signal.reshape(blocks, span...]
    all_gather x4 -> x0, waiting for transfers between devices: 53.4 us -> none  [the longest x1 22.7 us: on_device(): lax.all_gather(d_resid.astype(jnp.bfloat16), 'tensor', axis=0, tiled=True)]
  transfers between devices with their start and end apart: 12 -> 0, of which waited for: 10 -> 0; matrix products, arithmetic and copies ran while one was open for 27% -> 0% of each run, Pallas kernels for 1% -> 0%
where the time goes in v1:
time: 373 us; the launch traced here: 369 us
  Pallas kernels  337 us (90%)
  other arithmetic  16.6 us (4%)
  local copies, waits for them, and re-layouts  14 us (4%)
    pallas_call x4, Pallas kernels, run_stage(): pl.pallas_call(kernel, out_shape=tuple((jax.ShapeDtypeStruct(shape, kind)...  337 us
    convert_element_type x7, other arithmetic, finish(): gg, gu, gd, gao, gag, gv, gs, pk = (value.astype(f32) for value in sums)  12.8 us

profile of v1, /device:TPU:0, one launch (start us, length us, event | category | flops | bytes accessed | tf_op | source)
XLA Modules:
  0.0 368.6 jit_solution(7763318398284491633)
XLA Ops:
  0.7 0.8 compare_convert_fusion
  1.6 0.8 fusion.1
  2.4 0.7 constant_dynamic-update-slice_fusion.10
  3.1 0.7 constant_dynamic-update-slice_fusion.9
  3.9 0.8 constant_dynamic-update-slice_fusion.8
  4.6 0.8 constant_dynamic-update-slice_fusion.7
  5.4 0.7 constant_dynamic-update-slice_fusion.4
  6.1 0.7 constant_dynamic-update-slice_fusion.3
  6.8 0.7 constant_dynamic-update-slice_fusion.2
  7.5 0.7 constant_dynamic-update-slice_fusion.1
  8.3 0.7 constant_dynamic-update-slice_fusion
  9.0 1.0 broadcast_in_dim.24.refs_5_.refs_21_
  10.0 1.7 copy.43.refs_3_.refs_29_
  11.7 76.5 %shard_map.373 = (bf16[1024,1024]{1,0:T(8,128)(2,1)}, f32[2,1024,128]{2,1,0:T(8,128)}, f32[3,256,128]{2,1,0:T(8,128)}, f32[1024,256]{1,0:T(8,128)}, f32[16,8,8,1...) custom-call(bf16[256,1024]{1,0:T(8,128)(2,1)} %refs_24_.1, ...), custom_call_target="tpu_custom_call" | custom-call | tf_op jit(solution)/shard_map/pallas_call | solution.py:122
  88.2 47.6 %shard_map.374 = (bf16[640,1024]{1,0:T(8,128)(2,1)}, bf16[1024,640]{1,0:T(8,128)(2,1)}, bf16[1024,640]{1,0:T(8,128)(2,1)}, f32[256,1024]{1,0:T(8,128)}, f32[1,10...) custom-call(bf16[1024,1024]{1,0:T(8,128)(2,1)} %get-tuple-element.62.refs_0_, ...), custom_call_target="tpu_custom_call" | custom-call | tf_op jit(solution)/shard_map/pallas_call | solution.py:122
  135.7 62.1 %shard_map.375 = (bf16[512,1024]{1,0:T(8,128)(2,1)}, bf16[1024,512]{1,0:T(8,128)(2,1)}, bf16[1024,512]{1,0:T(8,128)(2,1)}, bf16[256,256]{1,0:T(8,128)(2,1)}, f32...) custom-call(bf16[1024,1024]{1,0:T(8,128)(2,1)} %get-tuple-element.67.refs_0_, bf16[512,1024]{1,0:T(8,128)(2,1)} %refs_1_.5, ...), custom_call_target="tpu_custom_call" | custom-call | tf_op jit(solution)/shard_map/pallas_call | solution.py:122
  197.8 150.8 %shard_map.376 = (bf16[1024,640]{1,0:T(8,128)(2,1)}, bf16[1024,640]{1,0:T(8,128)(2,1)}, bf16[640,1024]{1,0:T(8,128)(2,1)}, bf16[512,1024]{1,0:T(8,128)(2,1)}, bf...) custom-call(bf16[1024,640]{1,0:T(8,128)(2,1)} %get-tuple-element.87.refs_0_,, ...), custom_call_target="tpu_custom_call" | custom-call | tf_op jit(solution)/shard_map/pallas_call | solution.py:122
  348.6 1.4 fusion
  350.1 0.8 slice_bitcast_fusion.6
  350.8 1.4 slice_bitcast_fusion
  352.3 0.6 copy.46
  352.9 0.6 copy.45
  353.5 1.6 convert_element_type.29
  355.1 2.8 convert_element_type.30
  357.9 1.6 convert_element_type.31
  359.5 1.6 convert_element_type.32
  361.2 1.7 convert_element_type.33
  362.9 0.2 copy-done.1
  363.0 1.7 convert_element_type.34
  364.9 1.8 convert_element_type.35
  366.7 0.8 copy.59
  367.5 0.8 copy.60
  (19 shorter events, 0.4 us)
Async XLA Ops:
  9.0 2.7 copy-start.5
  348.6 9.3 %copy-start.4 = (bf16[1024,512]{1,0:T(8,128)(2,1)S(1)}, bf16[1024,512]{1,0:T(8,128)(2,1)}, u32[]{:S(2)}) copy-start(bf16[1024,512]{1,0:T(8,128)(2,1)} %get-tuple-element.98) | copy-start | bytes 3145732
  357.9 1.6 copy-start.3
  359.5 1.6 copy-start.2
  361.2 1.8 copy-start.1
  363.0 1.8 copy-start
  364.9 1.8 copy-start.6
  364.9 2.6 copy-start.7

commit v2 on v1

--- a/solution.py
+++ b/solution.py
@@ -19,7 +19,7 @@
 SPAN = 64
 MAX_DOC = 512
 PACK_TAIL = 32
-VMEM_BYTES = 60 * 2**20
+VMEM_BYTES = 62 * 2**20
 
 
 def plain(left, right):
@@ -47,19 +47,20 @@
 
 
 class Stage:
-    def __init__(self, ins, outs, scratch, refs):
+    def __init__(self, ins, outs, bare, scratch, refs):
         self.pending = {}
         self.flushed = []
         count = len(ins)
         self.hbm_in = dict(zip(ins, refs[:count]))
-        self.hbm_out = dict(zip(outs, refs[count : count + len(outs)]))
-        rest = refs[count + len(outs) :]
+        total = len(outs) + len(bare)
+        self.hbm_out = dict(zip(list(outs) + list(bare), refs[count : count + total]))
+        rest = refs[count + total :]
         names = list(ins) + list(outs) + list(scratch)
         self.refs = dict(zip(names, rest[: len(names)]))
         self.load_sem, self.flush_sem, self.send_sem, self.recv_sem = rest[len(names) :]
         self.order = {name: k for k, name in enumerate(ins)}
-        self.out_order = {name: k for k, name in enumerate(outs)}
-        self.used = 0
+        self.out_order = {name: k for k, name in enumerate(self.hbm_out)}
+        self.sends = self.receipts = 0
         self.names = {id(ref): name for name, ref in self.refs.items()}
 
     def __getitem__(self, name):
@@ -84,58 +85,68 @@
 
     def flush(self, *refs):
         for name in [self.names[id(ref)] for ref in refs]:
-            copy = pltpu.make_async_copy(
-                self.refs[name], self.hbm_out[name], self.flush_sem.at[self.out_order[name]]
-            )
-            copy.start()
-            self.flushed.append(copy)
+            self.store(self.refs[name], name)
+
+    def store(self, source, name):
+        copy = pltpu.make_async_copy(
+            source, self.hbm_out[name], self.flush_sem.at[self.out_order[name]]
+        )
+        copy.start()
+        self.flushed.append(copy)
 
     def close(self):
+        assert self.sends <= self.send_sem.shape[0]
+        assert self.receipts <= self.recv_sem.shape[0]
         for copy in self.flushed:
             copy.wait()
 
-    def sems(self, count):
-        first = self.used
-        self.used += count
+
+    def sems(self, count, sends=None):
+        first = self.sends, self.receipts
+        self.sends += count if sends is None else sends
+        self.receipts += count
         return first
 
-    def remote(self, source, target_ref, index, device):
+    def remote(self, source, target_ref, base, index, device, sent=None):
         return pltpu.make_async_remote_copy(
             src_ref=source,
             dst_ref=target_ref,
-            send_sem=self.send_sem.at[index],
-            recv_sem=self.recv_sem.at[index],
+            send_sem=self.send_sem.at[base[0] + (index if sent is None else sent)],
+            recv_sem=self.recv_sem.at[base[1] + index],
             device_id=device,
             device_id_type=MESH,
         )
 
 
-def run_stage(body, ins, outs, scratch, sems, collective):
+def run_stage(body, ins, outs, scratch, sems, collective, bare=()):
     ins = vars(ins)
+    written = {**outs, **dict(bare)}
 
     def kernel(*refs):
-        body(Stage(list(ins), list(outs), list(scratch), refs))
+        body(Stage(list(ins), list(outs), list(dict(bare)), list(scratch), refs))
 
     buffers = [pltpu.VMEM(array.shape, array.dtype) for array in ins.values()]
     buffers += [pltpu.VMEM(shape, kind) for shape, kind in outs.values()]
     buffers += [pltpu.VMEM(shape, kind) for shape, kind in scratch.values()]
     results = pl.pallas_call(
         kernel,
-        out_shape=tuple(jax.ShapeDtypeStruct(shape, kind) for shape, kind in outs.values()),
+        out_shape=tuple(jax.ShapeDtypeStruct(shape, kind) for shape, kind in written.values()),
         in_specs=[pl.BlockSpec(memory_space=pl.ANY)] * len(ins),
-        out_specs=tuple(pl.BlockSpec(memory_space=pl.ANY) for _ in outs),
+        out_specs=tuple(pl.BlockSpec(memory_space=pl.ANY) for _ in written),
         scratch_shapes=buffers
         + [
             pltpu.SemaphoreType.DMA((len(ins),)),
-            pltpu.SemaphoreType.DMA((len(outs),)),
-            pltpu.SemaphoreType.DMA((sems,)),
-            pltpu.SemaphoreType.DMA((sems,)),
+            pltpu.SemaphoreType.DMA((len(written),)),
+            pltpu.SemaphoreType.DMA((max(sems[0], 1),)),
+            pltpu.SemaphoreType.DMA((max(sems[1], 1),)),
         ],
         compiler_params=pltpu.CompilerParams(
-            collective_id=collective, has_side_effects=True, vmem_limit_bytes=VMEM_BYTES
+            collective_id=collective,
+            has_side_effects=collective is not None,
+            vmem_limit_bytes=VMEM_BYTES,
         ),
     )(*ins.values())
-    return types.SimpleNamespace(**dict(zip(outs, results)))
+    return types.SimpleNamespace(**dict(zip(written, results)))
 
 
 class Group:
@@ -147,11 +158,13 @@
         self.opp = (1 - chip) * 2 + core
         self.diag = (1 - chip) * 2 + (1 - core)
 
-    def greet(self):
+    def greet(self, more=()):
         barrier = pltpu.get_barrier_semaphore()
+        for device in more:
+            pl.semaphore_signal(barrier, inc=1, device_id={"dp": device}, device_id_type=MESH)
         for device in (self.sib, self.opp, self.diag):
             pl.semaphore_signal(barrier, inc=1, device_id={"tensor": device}, device_id_type=MESH)
-        pl.semaphore_wait(barrier, 3)
+        pl.semaphore_wait(barrier, 3 + len(more))
 
 
 class Gather:
@@ -162,14 +175,14 @@
         opp = {"tensor": group.opp}
         sib = {"tensor": group.sib}
         self.to_opp = [
-            stage.remote(source(s), place(group.me, s), base + s, opp) for s in range(pieces)
+            stage.remote(source(s), place(group.me, s), base, s, opp) for s in range(pieces)
         ]
         self.to_sib = [
-            stage.remote(source(s), place(group.me, s), base + pieces + s, sib)
+            stage.remote(source(s), place(group.me, s), base, pieces + s, sib)
             for s in range(pieces)
         ]
         self.passed = [
-            stage.remote(place(group.opp, s), place(group.opp, s), base + 2 * pieces + s, sib)
+            stage.remote(place(group.opp, s), place(group.opp, s), base, 2 * pieces + s, sib)
             for s in range(pieces)
         ]
 
@@ -209,14 +222,14 @@
         def copies(source, target, first, device):
             return [
                 stage.remote(
-                    source.at[self.part(s)], target.at[self.part(s)], first + s, {"tensor": device}
+                    source.at[self.part(s)], target.at[self.part(s)], base, first + s, {"tensor": device}
                 )
                 for s in range(pieces)
             ]
 
-        self.first = copies(self.out_diag, self.in_opp, base, group.sib)
-        self.second = copies(self.out_sib, self.in_own, base + pieces, group.sib)
-        self.across = copies(self.out_opp, self.in_far, base + 2 * pieces, group.opp)
+        self.first = copies(self.out_diag, self.in_opp, 0, group.sib)
+        self.second = copies(self.out_sib, self.in_own, pieces, group.sib)
+        self.across = copies(self.out_opp, self.in_far, 2 * pieces, group.opp)
 
     def part(self, s):
         return pl.ds(s * self.rows, self.rows)
@@ -288,13 +301,8 @@
         self.items = items
         self.place, self.seat = ring_seats(count)
         self.steps = 2 * (count - 1)
-        self.base = m.sems(len(items) * 2 * self.steps)
-        self.sent = []
-
-    def greet(self, barrier):
-        for step in (-1, 1):
-            device = self.seat(self.place + step)
-            pl.semaphore_signal(barrier, inc=1, device_id={"dp": device}, device_id_type=MESH)
+        self.base = m.sems(len(items) * 2 * count, len(items) * 2)
+        self.step = 0
 
     def view(self, ref, chunk, way):
         shape = ref.shape
@@ -307,47 +315,132 @@
         ]
 
     def copy(self, item, way, step):
-        own, box, total = self.items[item]
+        own, box, _ = self.items[item]
         sign = 1 - 2 * way
         last = self.count - 1
-        index = self.base + (2 * item + way) * self.steps + step
+        place = 2 * item + way
+        index = place * self.count + step % self.count
         if step < last:
             source = self.view(own, self.place, way) if step == 0 else box.at[way, step - 1]
             target = box.at[way, step]
         else:
-            source = self.view(total, self.place + sign - sign * (step - last), way)
+            source = self.view(own, self.place + sign - sign * (step - last), way)
             target = source
-        return self.m.remote(source, target, index, {"dp": self.seat(self.place + sign)})
+        device = {"dp": self.seat(self.place + sign)}
+        return self.m.remote(source, target, self.base, index, device, place)
 
     def start(self, item, way, step):
-        copy = self.copy(item, way, step)
-        copy.start()
-        self.sent.append(copy)
+        self.copy(item, way, step).start()
 
     def begin(self):
         for item in range(len(self.items)):
             for way in range(2):
                 self.start(item, way, 0)
 
-    def tick(self, step):
+    def tick(self):
         last = self.count - 1
-        for item, (own, box, total) in enumerate(self.items):
+        step = self.step
+        self.step = step + 1
+        for item, (own, box, name) in enumerate(self.items):
             for way in range(2):
                 sign = 1 - 2 * way
                 self.copy(item, way, step).wait_recv()
+                self.copy(item, way, step).wait_send()
                 if step < last:
-                    chunk = self.place - sign * (step + 1)
-                    value = box[way, step].astype(f32) + self.view(own, chunk, way)[...].astype(f32)
+                    chunk = self.view(own, self.place - sign * (step + 1), way)
+                    value = box[way, step].astype(f32) + chunk[...].astype(f32)
                     if step < last - 1:
                         box[way, step] = value.astype(box.dtype)
                     else:
-                        self.view(total, chunk, way)[...] = value.astype(total.dtype)
+                        chunk[...] = value.astype(own.dtype)
                 if step + 1 < self.steps:
                     self.start(item, way, step + 1)
+                if step >= last - 1:
+                    self.keep(own, name, self.place + sign - sign * (step + 1 - last), way)
+        return step + 1 == self.steps
+
+    def keep(self, own, name, chunk, way):
+        out = self.m.hbm_out[name]
+        sem = self.m.flush_sem.at[self.m.out_order[name]]
+        pltpu.make_async_copy(self.view(own, chunk, way), self.view(out, chunk, way), sem).start()
 
     def close(self):
-        for copy in self.sent:
+        for own, _, name in self.items:
+            sem = self.m.flush_sem.at[self.m.out_order[name]]
+            pltpu.make_async_copy(own, self.m.hbm_out[name], sem).wait()
+
+
+class Direct:
+    def __init__(self, m, count, items):
+        self.m = m
+        self.count = count
+        self.items = items
+        self.me = lax.axis_index("dp")
+        self.base = m.sems(2 * len(items) * (count - 1))
+        self.step = 0
+
+    def share(self, ref, index):
+        return ref.at[at(index, ref.shape[0] // self.count), :]
+
+    def copies(self, step):
+        made = []
+        for item, (own, box, total, _) in enumerate(self.items):
+            for r in range(1, self.count):
+                there = lax.rem(self.me + r, self.count)
+                index = (2 * item + step) * (self.count - 1) + r - 1
+                if step == 0:
+                    source, target = self.share(own, there), box.at[r - 1]
+                else:
+                    source = target = self.share(total, self.me)
+                made.append(self.m.remote(source, target, self.base, index, {"dp": there}))
+        return made
+
+    def begin(self):
+        for copy in self.copies(0):
+            copy.start()
+
+    def tick(self):
+        for copy in self.copies(self.step):
+            copy.wait_recv()
+        if self.step == 0:
+            for own, box, total, _ in self.items:
+                value = self.share(own, self.me)[...].astype(f32)
+                for r in range(self.count - 1):
+                    value = value + box[r].astype(f32)
+                self.share(total, self.me)[...] = value.astype(total.dtype)
+            for copy in self.copies(1):
+                copy.start()
+        self.step += 1
+        return self.step == 2
+
+    def close(self):
+        for copy in self.copies(0) + self.copies(1):
             copy.wait_send()
+        for _, _, total, name in self.items:
+            self.m.store(total, name)
+
+
+class Turns:
+    def __init__(self):
+        self.waiting = []
+        self.rings = []
+
+    def begin(self, ring):
+        ring.begin()
+        self.waiting.append(ring)
+        self.rings.append(ring)
+
+    def tick(self):
+        if self.waiting:
+            ring = self.waiting.pop(0)
+            if not ring.tick():
+                self.waiting.append(ring)
+
+    def close(self):
+        while self.waiting:
+            self.tick()
+        for ring in self.rings:
+            ring.close()
 
 
 def ring_box(shape, kind, count):
@@ -355,63 +448,16 @@
     return ((2, count - 1, rows, columns), kind)
 
 
-def run_ring(arrays, count, collective):
-    names = list(arrays)
-    outs = {name + "t": (array.shape, array.dtype) for name, array in arrays.items()}
-    scratch = {name + "b": ring_box(a.shape, a.dtype, count) for name, a in arrays.items()}
-
-    def body(m):
-        refs = [(m[name], m[name + "b"], m[name + "t"]) for name in names]
-        m.load(*[own for own, _, _ in refs])
-        ring = Ring(m, count, refs)
-        barrier = pltpu.get_barrier_semaphore()
-        ring.greet(barrier)
-        pl.semaphore_wait(barrier, 2)
-        m.need(*[own for own, _, _ in refs])
-        ring.begin()
-        for step in range(ring.steps):
-            ring.tick(step)
-        for _, _, total in refs:
-            m.flush(total)
-        ring.close()
-        m.close()
-
-    sems = len(names) * 4 * (count - 1)
-    done = run_stage(
-        body, types.SimpleNamespace(**arrays), outs, scratch, sems, collective
-    )
-    return [getattr(done, name + "t") for name in names]
-
-
-def sum_over_dp(arrays, collective):
-    count = lax.axis_size("dp")
-    if count > 1 and count % 2 == 0 and all(
-        ring_rows(a.shape, a.dtype, count) for a in arrays.values()
-    ):
-        return run_ring(arrays, count, collective)
-    return lax.psum([array.astype(f32) for array in arrays.values()], "dp")
-
-
-def tables_of(ema_alpha, ema_delta, ema_theta, ema_beta, eta_real, eta_imag):
-    magnitude = 1.0 - ema_alpha * ema_delta
-    cosine, sine = jnp.cos(ema_theta), jnp.sin(ema_theta)
-    scaled = ema_alpha * ema_beta
-    stacked = jnp.stack(
-        [
-            magnitude * cosine,
-            magnitude * sine,
-            scaled * eta_real,
-            scaled * eta_imag,
-            cosine,
-            sine,
-            ema_alpha,
-            ema_delta,
-            ema_beta,
-            eta_real,
-            eta_imag,
-        ]
-    )
-    return jnp.swapaxes(stacked, 1, 2)
+def direct_box(shape, kind, count):
+    return ((count - 1, shape[0] // count, shape[1]), kind)
+
+
+def ring_fits(shapes, count):
+    return (
+        count > 1
+        and count % 2 == 0
+        and all(ring_rows(shape, kind, count) for shape, kind in shapes)
+    )
 
 
 def groups(array):
@@ -478,16 +524,15 @@
                 value = value + m.part[l, pl.ds(s, SPAN, stride=SUB), :]
             gate = sigmoid(value)
             m.mxl[rows, lanes] = (value * gate).astype(bf16)
-            m.se[rows, lanes] = gate * (1.0 + value * (1.0 - gate))
+            m.se[rows, lanes] = (gate * (1.0 + value * (1.0 - gate))).astype(bf16)
         return state
 
     return lax.fori_loop(first, first + count, chunk, state)
 
 
 def window_mask(m, first_row, rows, first_key, keys):
-    same = m.segc[pl.ds(pl.multiple_of(first_row, LANES), rows), :] == m.segr[
-        :, pl.ds(pl.multiple_of(first_key, LANES), keys)
-    ]
+    here = m.segb[pl.ds(pl.multiple_of(first_row + SUB, SUB), rows), :][:, :1]
+    same = here == m.segr[:, pl.ds(pl.multiple_of(first_key, LANES), keys)].astype(f32)
     row = first_row + lax.broadcasted_iota(jnp.int32, (rows, keys), 0)
     key = first_key + lax.broadcasted_iota(jnp.int32, (rows, keys), 1)
     return same & (row >= key)
@@ -499,6 +544,34 @@
     first = jnp.maximum(index - back, 0) * block
     first = jnp.minimum(first, length - keys)
     return pl.multiple_of(first, LANES), keys
+
+
+def keeping(m):
+    length = m.segr.shape[1]
+    m.segb[:SUB, :] = jnp.full((SUB, LANES), -1.0, f32)
+    for k in range(length // LANES):
+        row = m.segr[:, k * LANES : (k + 1) * LANES].astype(f32)
+        m.segb[SUB + k * LANES : SUB + (k + 1) * LANES, :] = jnp.broadcast_to(row, (LANES, LANES)).T
+    for k in range(length // LANES):
+        now = m.segb[SUB + k * LANES : SUB + (k + 1) * LANES, :]
+        before = m.segb[SUB - 1 + k * LANES : SUB - 1 + (k + 1) * LANES, :]
+        m.kf[k * LANES : (k + 1) * LANES, :] = jnp.where(now == before, 1.0, 0.0)
+    m.kf[length:, :] = jnp.zeros((SUB, LANES), f32)
+
+
+def filter_tables(m):
+    alpha, delta, theta, beta, e_re, e_im = (
+        ref[...] for ref in (m.p0, m.p1, m.p2, m.p3, m.p4, m.p5)
+    )
+    magnitude = 1.0 - alpha * delta
+    cosine, sine = jnp.cos(theta), jnp.sin(theta)
+    scaled = alpha * beta
+    entries = (
+        magnitude * cosine, magnitude * sine, scaled * e_re, scaled * e_im,
+        cosine, sine, alpha, delta, beta, e_re, e_im,
+    )
+    for k, entry in enumerate(entries):
+        m.tab[k] = entry
 
 
 def body_a(m):
@@ -508,7 +581,8 @@
     blocks = length // block
     channels = m.mxl.shape[1]
     sides = channels // LANES
-    m.load(m.tok, m.wsh, m.kf, m.segc, m.segr, m.gain, m.tab, m.om, m.wv, m.cot, m.wag)
+    m.load(m.tok, m.wsh, m.cot, m.segr, m.p0, m.p1, m.p2, m.p3, m.p4, m.p5)
+    m.load(m.gain, m.om, m.wv, m.wag)
     m.load(m.qg, m.qb, m.kg, m.wo, m.rg)
     g.greet()
 
@@ -521,7 +595,7 @@
         2,
     )
     shared = Gather(m, g, lambda s: m.wsh, lambda j, s: m.wsf.at[at(j, channels), :], 1)
-    pieces = 4
+    pieces = 8
     rows_piece = length // pieces
     mixed = Gather(
         m, g,
@@ -547,9 +621,14 @@
     tokens.send(0)
     tokens.send(1)
     shared.send(0)
+    m.need(m.cot)
+    cots.send(0)
     m.xt[own, :] = m.tok[...]
     m.wsf[at(g.me, channels), :] = m.wsh[...]
-    m.need(m.kf, m.segc, m.segr, m.gain, m.tab, m.om)
+    m.need(m.segr, m.p0, m.p1, m.p2, m.p3, m.p4, m.p5, m.gain, m.om)
+    keeping(m)
+    filter_tables(m)
+    m.flush(m.kf, m.segb, m.tab)
 
     lane = lax.broadcasted_iota(jnp.int32, (SPAN, LANES), 1)
 
@@ -579,7 +658,6 @@
     sums(g.sib)
     tokens.forward(0)
     tokens.forward(1)
-    shared.forward(0)
     sums(g.opp)
     tokens.far()
     sums(g.diag)
@@ -632,8 +710,6 @@
         mixed.send(p)
         if p >= 2:
             mixed.forward(p - 2)
-    m.need(m.cot)
-    cots.send(0)
     cots.send(1)
     m.flush(m.se, m.st)
     for i in range(pieces):
@@ -655,6 +731,7 @@
     m.flush(m.v, m.sv)
     for p in range(max(pieces - 2, 0), pieces):
         mixed.forward(p)
+    shared.forward(0)
     shared.near()
     shared.far()
     mixed.near()
@@ -664,7 +741,7 @@
     def project(i, _):
         rows = at(i, block)
         z = plain(m.mx[rows, :], m.wsf[...])
-        m.z[rows, :] = z
+        m.z[rows, :] = z.astype(bf16)
         m.q[rows, :] = (z * m.qg[...] + m.qb[...]).astype(bf16)
         m.k[rows, :] = (z * m.kg[...]).astype(bf16)
         return 0
@@ -692,10 +769,10 @@
         return plain(m.w[rows, :], m.wo[...])
 
     branch.put_diag(pieces_of(attend(g.diag), 2))
+    branch.put_opp(pieces_of(attend(g.opp), 2))
     cots.forward(0)
+    branch.put_sib(pieces_of(attend(g.sib), 2))
     cots.forward(1)
-    branch.put_opp(pieces_of(attend(g.opp), 2))
-    branch.put_sib(pieces_of(attend(g.sib), 2))
     m.bp[...] = attend(g.me)
     m.flush(m.p, m.r, m.os, m.w)
     for s in range(2):
@@ -726,17 +803,21 @@
     blocks = length // block
     keys = min((-(-MAX_DOC // block) + 1) * block, length)
     sides = channels // LANES
-    states = 2 * sides * (arrays.tab.shape[1] // SUB)
+    dims = arrays.p0.shape[0]
+    states = 2 * sides * (dims // SUB)
     outs = dict(
         xn=((length, width), bf16),
         xl=((sides, length, LANES), f32),
+        tab=((11, dims, channels), f32),
+        kf=((length + SUB, LANES), f32),
+        segb=((length + SUB, LANES), f32),
         so=((3, block, LANES), f32),
-        se=((length, channels), f32),
+        se=((length, channels), bf16),
         st=((length // SPAN, states, SUB, LANES), f32),
         mx=((length, width), bf16),
         v=((length, values), bf16),
         sv=((length, values), bf16),
-        z=((length, shared), f32),
+        z=((length, shared), bf16),
         q=((length, shared), bf16),
         k=((length, shared), bf16),
         wsf=((width, shared), bf16),
@@ -761,17 +842,16 @@
         yno=((block, width), bf16),
         **scatter_buffers("br", block, width),
     )
-    return run_stage(body_a, arrays, outs, scratch, 64, 1)
-
-
-def transposed_product(m, left, right, out, step):
+    return run_stage(body_a, arrays, outs, scratch, (51, 51), 1)
+
+
+def transposed_product(left, right, out, step):
     def part(i, _):
         columns = at(i, step)
         out[columns, :] = inner(left[:, columns], right[...]).astype(bf16)
         return 0
 
     lax.fori_loop(0, left.shape[1] // step, part, 0)
-    m.flush(out)
 
 
 def body_b(m):
@@ -782,13 +862,6 @@
     m.load(m.yn, m.wg, m.wu, m.wd, m.cotf, m.y, m.rs, m.cot, m.rg)
     g.greet()
     grads = Scatter(m, g, "dy", 2)
-    fed = Scatter(m, g, "ff", 2)
-    back = Gather(
-        m, g,
-        lambda s: m.dyo.at[pl.ds(s * half, half), :],
-        lambda j, s: m.dyf.at[pl.ds(pl.multiple_of(j * block + s * half, half), half), :],
-        2,
-    )
     m.need(m.yn, m.wg, m.wu, m.wd, m.cotf)
 
     def feed(j):
@@ -808,7 +881,13 @@
     grads.put_opp(pieces_of(feed(g.opp), 2))
     grads.put_sib(pieces_of(feed(g.sib), 2))
     m.bp[...] = feed(g.me)
-    transposed_product(m, m.act, m.cotf, m.gd, LANES)
+    m.flush(m.act)
+    transposed_product(m.act, m.cotf, m.gd, LANES)
+    m.flush(m.gd)
+    transposed_product(m.yn, m.dg, m.gg, 2 * LANES)
+    m.flush(m.gg)
+    transposed_product(m.yn, m.du, m.gu, 2 * LANES)
+    m.flush(m.gu)
     m.need(m.y, m.rs, m.cot, m.rg)
     gain_sum = jnp.zeros((1, width), f32)
     for s in range(2):
@@ -822,28 +901,9 @@
         dy = m.cot[piece, :].astype(f32) + rms * pull
         m.dy[piece, :] = dy
         m.dyo[piece, :] = dy.astype(bf16)
-        back.send(s)
     m.gr[...] = gain_sum
-    m.dyf[at(g.me, block), :] = m.dyo[...]
-    m.flush(m.dy, m.gr)
-    share = lambda j: plain(m.act[at(j, block), :], m.wd[...])
-    fed.put_diag(pieces_of(share(g.diag), 2))
-    fed.put_opp(pieces_of(share(g.opp), 2))
-    fed.put_sib(pieces_of(share(g.sib), 2))
-    m.bp[...] = share(g.me)
-    transposed_product(m, m.yn, m.dg, m.gg, 2 * LANES)
-    back.forward(0)
-    back.forward(1)
-    transposed_product(m, m.yn, m.du, m.gu, 2 * LANES)
-    back.near()
-    back.far()
-    m.flush(m.dyf)
-    for s in range(2):
-        piece = pl.ds(s * half, half)
-        m.out[piece, :] = (fed.take(s, m.bp[piece, :]) + m.y[piece, :]).astype(bf16)
-    m.flush(m.out)
-    for moved in (grads, fed, back):
-        moved.close()
+    m.flush(m.dyo, m.dy, m.gr)
+    grads.close()
     m.close()
 
 
@@ -855,19 +915,16 @@
         gu=((width, units), bf16),
         dy=((block, width), f32),
         gr=((1, width), f32),
-        dyf=((length, width), bf16),
-        out=((block, width), bf16),
+        dyo=((block, width), bf16),
+        act=((length, units), bf16),
     )
     scratch = dict(
-        act=((length, units), bf16),
         dg=((length, units), bf16),
         du=((length, units), bf16),
         bp=((block, width), f32),
-        dyo=((block, width), bf16),
         **scatter_buffers("dy", block, width),
-        **scatter_buffers("ff", block, width),
-    )
-    return run_stage(body_b, arrays, outs, scratch, 32, 2)
+    )
+    return run_stage(body_b, arrays, outs, scratch, (6, 6), 2)
 
 
 def filter_backward(m, last, count, gamma):
@@ -904,7 +961,7 @@
                 t = ch * SPAN + local
                 keep = spread_row(m.kf, (pl.ds(t + 1, 1), slice(None)))
                 signals = [
-                    spread_row(m.de, (l, pl.ds(t, 1), slice(None))) for l in range(sides)
+                    spread_row(m.dq, (l, pl.ds(t, 1), slice(None))) for l in range(sides)
                 ]
                 _, gamma = advance(gamma, (root_real, root_imag), keep, signals, sides)
                 for l in range(sides):
@@ -928,7 +985,7 @@
         rows = at(ch, SPAN)
         for l in range(sides):
             lanes = slice(LANES * l, LANES * l + LANES)
-            signal = m.de[l, rows, :]
+            signal = m.dq[l, rows, :]
             value = m.om[:, lanes] * signal
             for s in range(SUB):
                 value = value + m.part[l, pl.ds(s, SPAN, stride=SUB), :]
@@ -968,42 +1025,92 @@
         m.pk[5 * dims + SUB * s : 5 * dims + SUB * s + SUB, lanes] = -scaled * f_im
 
 
-def body_c(m):
+def body_c(count, m):
     g = Group()
-    length, width = m.dyf.shape
+    length, width = m.mx.shape
     block = m.tok.shape[0]
     blocks = length // block
     half = block // 2
     channels = m.se.shape[1]
     shared = m.q.shape[1]
     sides = channels // LANES
-    m.load(m.dyf, m.wo, m.r, m.os, m.v, m.p, m.k, m.q, m.z, m.qg, m.kg, m.sv, m.wsf, m.wag)
-    m.load(m.wv, m.w, m.mx, m.xn, m.se, m.st, m.xl, m.kf, m.tab, m.om, m.tok, m.so, m.gain)
-    m.load(m.dy, m.gr, m.segc, m.segr)
-    g.greet()
+    m.load(m.dyo, m.gd, m.gg, m.gu, m.act, m.wd, m.w, m.wo, m.r, m.os, m.v, m.p, m.k, m.q, m.z)
+    m.load(m.qg, m.kg, m.sv, m.wsf, m.wag, m.wv, m.y, m.mx, m.xn, m.se, m.st, m.xl, m.kf, m.tab)
+    m.load(m.om, m.tok, m.so, m.gain, m.dy, m.gr, m.segb, m.segr)
+    turns = Turns()
+    down = inward = outer = tail = None
+    if count:
+        down = Ring(m, count, [(m.gd, m.gdb, "gdt")])
+        inward = Ring(m, count, [(m.gg, m.ggb, "ggt"), (m.gu, m.gub, "gut")])
+        outer = Ring(
+            m, count, [(m.gao, m.gaob, "gaot"), (m.r, m.gagb, "gagt"), (m.os, m.gvb, "gvt")]
+        )
+        tail = Direct(
+            m, count, [(m.gs, m.gsb, m.gss, "gst"), (m.pk, m.pkb, m.pks, "pkt")]
+        )
+        here = lax.axis_index("dp")
+        g.greet([lax.rem(here + r, count) for r in range(1, count)])
+    else:
+        g.greet()
+    fed = Scatter(m, g, "xv", 2)
+    back = Gather(
+        m, g,
+        lambda s: m.dyo.at[pl.ds(s * half, half), :],
+        lambda j, s: m.dyf.at[pl.ds(pl.multiple_of(j * block + s * half, half), half), :],
+        2,
+    )
+    m.need(m.dyo, m.gd, m.gg, m.gu)
+    back.send(0)
+    back.send(1)
+    m.dyf[at(g.me, block), :] = m.dyo[...]
+
+    def begin(ring, *pairs):
+        if ring is None:
+            for ref, name in pairs:
+                m.store(ref, name)
+        else:
+            turns.begin(ring)
+
+    begin(down, (m.gd, "gdt"))
+    begin(inward, (m.gg, "ggt"), (m.gu, "gut"))
     pieces = 4
     dm = Scatter(m, g, "dm", pieces, range(pieces - 1, -1, -1))
-    xv = Scatter(m, g, "xv", 2)
     sh = Scatter(m, g, "sh", 1)
     others = (g.sib, g.opp, g.diag)
     base = m.sems(9)
     parts = [
-        m.remote(m.dxb.at[at(dev, block), :], m.dxr.at[k], base + k, {"tensor": dev})
+        m.remote(m.dxb.at[at(dev, block), :], m.dxr.at[k], base, k, {"tensor": dev})
         for k, dev in enumerate(others)
     ]
     small = [
-        m.remote(m.smo, m.sm.at[g.me], base + 3 + k, {"tensor": dev})
+        m.remote(m.smo, m.sm.at[g.me], base, 3 + k, {"tensor": dev})
         for k, dev in enumerate(others)
     ]
     tails = [
-        m.remote(m.aro, m.ar.at[:, at(g.me, block)], base + 6 + k, {"tensor": dev})
+        m.remote(m.aro, m.ar.at[:, at(g.me, block)], base, 6 + k, {"tensor": dev})
         for k, dev in enumerate(others)
     ]
 
     scale = 1.0 / math.sqrt(shared)
     m.dk[...] = jnp.zeros(m.dk.shape, f32)
     m.dv[...] = jnp.zeros(m.dv.shape, f32)
-    m.need(m.dyf, m.wo, m.r, m.os, m.v, m.p, m.k, m.q)
+    m.need(m.act, m.wd)
+    share = lambda j: plain(m.act[at(j, block), :], m.wd[...])
+    fed.put_diag(pieces_of(share(g.diag), 2))
+    fed.put_sib(pieces_of(share(g.sib), 2))
+    m.dxn[...] = share(g.me)
+    turns.tick()
+    turns.tick()
+    back.forward(0)
+    turns.tick()
+    back.forward(1)
+    fed.put_opp(pieces_of(share(g.opp), 2))
+    turns.tick()
+    back.near()
+    back.far()
+    m.need(m.w, m.wo, m.r, m.os, m.v, m.p, m.k, m.q)
+    transposed_product(m.w, m.dyf, m.gao, 2 * LANES)
+    turns.tick()
 
     def attend(i, _):
         rows = at(i, block)
@@ -1017,17 +1124,22 @@
         weighed = prob * cross(d_o, m.v[window, :])
         d_s = (weighed - prob * jnp.sum(weighed, axis=1, keepdims=True)) * scale
         d_s = d_s.astype(bf16)
-        m.dq[rows, :] = plain(d_s, m.k[window, :])
+        d_q = plain(d_s, m.k[window, :])
+        for l in range(shared // LANES):
+            m.dq[l, rows, :] = d_q[:, LANES * l : LANES * l + LANES]
         m.dk[window, :] = m.dk[window, :] + inner(d_s, m.q[rows, :])
         m.dv[window, :] = m.dv[window, :] + inner(prob_low, d_o)
         return 0
 
-    lax.fori_loop(0, blocks, attend, 0)
+    for n in range(blocks):
+        attend(n, 0)
+        turns.tick()
     m.need(m.z, m.qg, m.kg, m.sv, m.wsf, m.wag)
 
     def affine(i, sums):
         rows = at(i, block)
-        d_q, d_k, z = m.dq[rows, :], m.dk[rows, :], m.z[rows, :]
+        d_q = jnp.concatenate([m.dq[l, rows, :] for l in range(shared // LANES)], axis=1)
+        d_k, z = m.dk[rows, :], m.z[rows, :].astype(f32)
         m.dz[rows, :] = (d_q * m.qg[...] + d_k * m.kg[...]).astype(bf16)
         m.dvp[rows, :] = (m.dv[rows, :] * m.sv[rows, :].astype(f32)).astype(bf16)
         new = (d_q * z, d_q, d_k * z)
@@ -1047,24 +1159,42 @@
 
         return value
 
+    m.need(m.y)
+    for s in range(2):
+        piece = pl.ds(s * half, half)
+        m.out[piece, :] = (fed.take(s, m.dxn[piece, :]) + m.y[piece, :]).astype(bf16)
+    m.flush(m.out)
+    fed.close()
+    m.need(m.mx, m.xn)
+    transposed_product(m.mx, m.drp, m.r, 2 * LANES)
+    turns.tick()
+    transposed_product(m.xn, m.dvp, m.os, 2 * LANES)
+    begin(outer, (m.gao, "gaot"), (m.r, "gagt"), (m.os, "gvt"))
     dm.put_diag(mixing(g.diag))
+    turns.tick()
     dm.put_opp(mixing(g.opp))
+    turns.tick()
     dm.put_sib(mixing(g.sib))
+    turns.tick()
     m.need(m.wv)
+    xv = Scatter(m, g, "xv", 2)
     spread = lambda j: pieces_of(cross(m.dvp[at(j, block), :], m.wv[...]), 2)
-    xv.put_diag(spread(g.diag))
-    xv.put_opp(spread(g.opp))
-    xv.put_sib(spread(g.sib))
-    m.dxn[...] = cross(m.dvp[at(g.me, block), :], m.wv[...])
-    m.need(m.w, m.mx, m.xn)
-    transposed_product(m, m.w, m.dyf, m.gao, 2 * LANES)
-    transposed_product(m, m.mx, m.drp, m.gag, 2 * LANES)
-    transposed_product(m, m.xn, m.dvp, m.gv, 2 * LANES)
     split = lambda j: (lambda s: inner(m.mx[:, at(j, channels)], m.dz[...]))
-    sh.put_diag(split(g.diag))
-    sh.put_opp(split(g.opp))
-    sh.put_sib(split(g.sib))
-    m.shp[...] = split(g.me)(0)
+
+    def spreading():
+        xv.put_diag(spread(g.diag))
+        xv.put_opp(spread(g.opp))
+        turns.tick()
+        xv.put_sib(spread(g.sib))
+        m.dxn[...] = cross(m.dvp[at(g.me, block), :], m.wv[...])
+        turns.tick()
+        sh.put_diag(split(g.diag))
+        sh.put_opp(split(g.opp))
+        turns.tick()
+        sh.put_sib(split(g.sib))
+        m.shp[...] = split(g.me)(0)
+        turns.tick()
+
     m.need(m.se, m.st, m.xl, m.kf, m.tab, m.om)
     half_states = m.acc.shape[0] // 4
     m.acc[...] = jnp.zeros(m.acc.shape, f32)
@@ -1074,23 +1204,27 @@
     own_mix = mixing(g.me)
     for s in range(pieces - 1, -1, -1):
         rows = pl.ds(s * (length // pieces), length // pieces)
-        d_e = dm.take(s, own_mix(s)) * m.se[rows, :]
+        d_e = dm.take(s, own_mix(s)) * m.se[rows, :].astype(f32)
         for l in range(sides):
-            m.de[l, rows, :] = d_e[:, LANES * l : LANES * l + LANES]
-        gamma = filter_backward(m, (s + 1) * per - 1, per, gamma)
+            m.dq[l, rows, :] = d_e[:, LANES * l : LANES * l + LANES]
+        for n in range(per - 1, -1, -1):
+            gamma = filter_backward(m, s * per + n, 1, gamma)
+            turns.tick()
         for k, dev in enumerate(others):
 
             @pl.when(dev == s)
             def _():
                 parts[k].start()
 
+        if s == pieces - 1:
+            spreading()
     filter_gradients(m)
     base_row = m.pk.shape[0] - PACK_TAIL
     m.pk[base_row:, :] = jnp.zeros((PACK_TAIL, channels), f32)
     m.pk[base_row : base_row + 1, :] = m.go[...]
     m.gs[...] = sh.take(0, m.shp[...]).astype(bf16)
-    m.flush(m.gs)
-    m.need(m.tok, m.so, m.gain, m.dy, m.gr, m.segc, m.segr)
+    turns.tick()
+    m.need(m.tok, m.so, m.gain, m.dy, m.gr, m.segb, m.segr)
     for s in range(2):
         piece = pl.ds(s * half, half)
         m.dxn[piece, :] = xv.take(s, m.dxn[piece, :])
@@ -1130,11 +1264,12 @@
         copy.start()
     m.ar[:, at(g.me, block)] = m.aro[...]
     m.sm[g.me] = m.smo[...]
-    back = -(-MAX_DOC // block)
-    keys = min((back + 1) * block, length)
+    reach = -(-MAX_DOC // block)
+    keys = min((reach + 1) * block, length)
     first_key = pl.multiple_of(jnp.minimum(g.me * block, length - keys), LANES)
     first_row = pl.multiple_of(g.me * block, LANES)
-    same = m.segc[pl.ds(first_row, block), :] == m.segr[:, pl.ds(first_key, keys)]
+    here = m.segb[pl.ds(pl.multiple_of(first_row + SUB, SUB), block), :][:, :1]
+    same = here == m.segr[:, pl.ds(first_key, keys)].astype(f32)
     row = first_row + lax.broadcasted_iota(jnp.int32, (block, keys), 0)
     key = first_key + lax.broadcasted_iota(jnp.int32, (block, keys), 1)
     seen = (same & (row <= key)).astype(bf16)
@@ -1149,6 +1284,7 @@
         x = m.tok[piece, :].astype(f32)
         m.gt[piece, :] = (m.dxn[piece, :] + b_one[rows] + 2.0 * x * b_two[rows]).astype(bf16)
     m.flush(m.gt)
+    turns.tick()
     for copy in small:
         copy.wait_recv()
     total = m.sm[0]
@@ -1162,30 +1298,45 @@
     for n in range(3):
         row = base_row + 1 + 2 * per + n
         m.pk[row : row + 1, :shared] = total[2 + n : 3 + n, :shared]
-    m.flush(m.pk)
-    for moved in (dm, xv, sh):
+    begin(tail, (m.gs, "gst"), (m.pk, "pkt"))
+    turns.close()
+    for moved in (dm, xv, sh, back):
         moved.close()
     for copy in parts + small + tails:
         copy.wait_send()
     m.close()
 
 
-def run_c(arrays, sizes):
+def run_c(arrays, sizes, count):
     length, width, block, channels, shared, values = sizes
+    units = arrays.act.shape[1]
     sides = channels // LANES
-    half_states = sides * (arrays.tab.shape[1] // SUB)
-    outs = dict(
+    dims = arrays.tab.shape[1]
+    half_states = sides * (dims // SUB)
+    late = dict(
         gao=((values, width), bf16),
         gag=((width, values), bf16),
         gv=((width, values), bf16),
         gs=((channels, shared), bf16),
-        pk=((6 * arrays.tab.shape[1] + PACK_TAIL, channels), f32),
+        pk=((6 * dims + PACK_TAIL, channels), f32),
+    )
+    summed = dict(
+        gd=((units, width), bf16),
+        gg=((width, units), bf16),
+        gu=((width, units), bf16),
+        **late,
+    )
+    if not ring_fits(summed.values(), count):
+        count = 0
+    outs = dict(
         gt=((block, width), bf16),
+        out=((block, width), bf16),
     )
     scratch = dict(
+        dyf=((length, width), bf16),
         dk=((length, shared), f32),
         dv=((length, values), f32),
-        dq=((length, shared), f32),
+        dq=((max(sides, shared // LANES), length, LANES), f32),
         drp=((length, values), bf16),
         dz=((length, shared), bf16),
         dvp=((length, values), bf16),
@@ -1195,7 +1346,6 @@
         acc=((4 * half_states, SUB, LANES), f32),
         kept=((SPAN, 2 * half_states, SUB, LANES), f32),
         part=((sides, SPAN * SUB, LANES), f32),
-        de=((sides, length, LANES), f32),
         dxb=((length, channels), bf16),
         dxr=((3, block, channels), bf16),
         aw=((block, LANES), f32),
@@ -1204,31 +1354,97 @@
         ar=((16, length), bf16),
         smo=((SUB, width), f32),
         sm=((length // block, SUB, width), f32),
+        **{name: late[name] for name in ("gao", "gs", "pk")},
         **scatter_buffers("dm", length, channels),
         **scatter_buffers("xv", block, width),
         **scatter_buffers("sh", channels, shared),
     )
-    done = run_stage(body_c, arrays, outs, scratch, 48, 3)
-    done.dims = arrays.tab.shape[1]
+    sems = [42, 42]
+    if count:
+        for name, (shape, kind) in summed.items():
+            small = name in ("gs", "pk")
+            scratch[name + "b"] = (direct_box if small else ring_box)(shape, kind, count)
+        scratch.update(gss=summed["gs"], pks=summed["pk"])
+        sems = [42 + 12 + 4 * (count - 1), 42 + 12 * count + 4 * (count - 1)]
+    bare = {name + "t": entry for name, entry in summed.items()}
+    done = run_stage(
+        functools.partial(body_c, count), arrays, outs, scratch, sems, 3, bare.items()
+    )
+    done.dims = dims
+    done.summed = bool(count)
     return done
 
 
-def finish(a, b, c, shared):
-    sums = sum_over_dp(
-        dict(gg=b.gg, gu=b.gu, gd=b.gd, gao=c.gao, gag=c.gag, gv=c.gv, gs=c.gs, pk=c.pk), 4
-    )
-    gg, gu, gd, gao, gag, gv, gs, pk = (value.astype(f32) for value in sums)
-    dims = c.dims
-    tables = [pk[dims * k : dims * k + dims].T for k in range(6)]
+def body_f(dims, shared, m):
+    wide = ((m.gd, m.gdt), (m.gg, m.ggt), (m.gu, m.gut), (m.gao, m.gaot), (m.gag, m.gagt))
+    wide += ((m.gv, m.gvt), (m.gs, m.gst))
+    m.load(m.out, m.gt, m.gd, m.gg, m.gu, m.gao, m.gag, m.gv, m.gs, m.pk)
+    for source, target in ((m.out, m.outt), (m.gt, m.gtt)):
+        m.need(source)
+        target[...] = source[...]
+        m.flush(target)
+    for source, target in wide:
+        m.need(source)
+        rows = source.shape[0] // 2
+        for n in range(2):
+
+            def part(i, _):
+                piece = pl.ds(pl.multiple_of(n * rows + i * 16, 16), 16)
+                target[piece, :] = source[piece, :].astype(f32)
+                return 0
+
+            lax.fori_loop(0, rows // 16, part, 0, unroll=4)
+        m.flush(target)
+    m.need(m.pk)
+    for k, out in enumerate((m.e0, m.e1, m.e2, m.e3, m.e4, m.e5)):
+        out[...] = m.pk[k * dims : (k + 1) * dims, :]
     top = 6 * dims
-    width = gao.shape[1]
-    per = width // pk.shape[1]
-    norm = pk[top + 1 : top + 1 + per].reshape(width)
-    rms = pk[top + 1 + per : top + 1 + 2 * per].reshape(width)
-    aff = pk[top + 1 + 2 * per :, :shared]
+    channels = m.pk.shape[1]
+    m.om[...] = m.pk[top : top + 1, :]
+    per = m.norm.shape[1] // channels
+    for n, out in enumerate((m.norm, m.rms)):
+        for k in range(per):
+            row = top + 1 + n * per + k
+            out[:, k * channels : (k + 1) * channels] = m.pk[row : row + 1, :]
+    for n, out in enumerate((m.qg, m.qb, m.kg)):
+        row = top + 1 + 2 * per + n
+        out[...] = m.pk[row : row + 1, :shared]
+    m.flush(m.e0, m.e1, m.e2, m.e3, m.e4, m.e5, m.om, m.norm, m.rms, m.qg, m.qb, m.kg)
+    m.close()
+
+
+def finish(c, shared):
+    sums = dict(gd=c.gdt, gg=c.ggt, gu=c.gut, gao=c.gaot, gag=c.gagt, gv=c.gvt, gs=c.gst, pk=c.pkt)
+    if not c.summed:
+        total = lax.psum([value.astype(f32) for value in sums.values()], "dp")
+        sums = {name: v.astype(old.dtype) for (name, old), v in zip(sums.items(), total)}
+    channels, width = sums["pk"].shape[1], sums["gd"].shape[1]
+    outs = dict(
+        e0=((c.dims, channels), f32),
+        e1=((c.dims, channels), f32),
+        e2=((c.dims, channels), f32),
+        e3=((c.dims, channels), f32),
+        e4=((c.dims, channels), f32),
+        e5=((c.dims, channels), f32),
+        om=((1, channels), f32),
+        norm=((1, width), f32),
+        rms=((1, width), f32),
+        qg=((1, shared), f32),
+        qb=((1, shared), f32),
+        kg=((1, shared), f32),
+    )
+    for name, value in sums.items():
+        if value is not sums["pk"]:
+            outs[name + "t"] = (value.shape, f32)
+    outs.update(outt=(c.out.shape, bf16), gtt=(c.gt.shape, bf16))
+    f = run_stage(
+        functools.partial(body_f, c.dims, shared),
+        types.SimpleNamespace(out=c.out, gt=c.gt, **sums), outs, {}, (0, 0), None,
+    )
+    tables = [table.T for table in (f.e0, f.e1, f.e2, f.e3, f.e4, f.e5)]
     return (
-        b.out, c.gt, norm, *tables, pk[top], gs, aff[0], aff[1], aff[2], gag, gv, gao,
-        rms, gg, gu, gd,
+        f.outt, f.gtt, f.norm[0], *tables, f.om[0], f.gst,
+        f.qg[0], f.qb[0], f.kg[0], f.gagt, f.gvt, f.gaot, f.rms[0], f.ggt, f.gut, f.gdt,
     )
 
 
@@ -1262,18 +1478,15 @@
     shared = w_shared.shape[1]
     values = w_value.shape[1]
     units = w_gate.shape[1]
-    tab = tables_of(ema_alpha, ema_delta, ema_theta, ema_beta, eta_real, eta_imag)
     om = ema_omega[None]
     gain, rg = timestep_norm_gain[None], rms_gain[None]
     qg, qb, kg = q_gain[None], q_bias[None], k_gain[None]
-    segc, segr = segments.reshape(length, 1), segments
-    keep = (segments[0, 1:] == segments[0, :-1]).astype(f32)
-    keep = jnp.concatenate([jnp.zeros((1,), f32), keep, jnp.zeros((SUB,), f32)])
-    kf = jnp.broadcast_to(keep[:, None], (length + SUB, LANES))
+    segr = segments
     a = run_a(
         types.SimpleNamespace(
-            tok=tokens, cot=cotangent, wsh=w_shared, segc=segc, segr=segr, kf=kf, gain=gain,
-            tab=tab, om=om, qg=qg, qb=qb, kg=kg, wag=w_attgate, wv=w_value, wo=w_attout, rg=rg,
+            tok=tokens, cot=cotangent, wsh=w_shared, segr=segr, gain=gain,
+            p0=ema_alpha.T, p1=ema_delta.T, p2=ema_theta.T,
+            p3=ema_beta.T, p4=eta_real.T, p5=eta_imag.T, om=om, qg=qg, qb=qb, kg=kg, wag=w_attgate, wv=w_value, wo=w_attout, rg=rg,
         ),
         (length, width, block, channels, shared, values),
     )
@@ -1286,15 +1499,17 @@
     )
     c = run_c(
         types.SimpleNamespace(
-            dyf=b.dyf, wo=w_attout, r=a.r, os=a.os, v=a.v, p=a.p, k=a.k,
+            dyo=b.dyo, gd=b.gd, gg=b.gg, gu=b.gu, act=b.act, wd=w_down, y=a.y,
+            wo=w_attout, r=a.r, os=a.os, v=a.v, p=a.p, k=a.k,
             q=a.q, z=a.z, qg=qg, kg=kg, sv=a.sv, wsf=a.wsf, wag=w_attgate,
             wv=w_value, w=a.w, mx=a.mx, xn=a.xn, se=a.se, st=a.st, xl=a.xl,
-            kf=kf, tab=tab, om=om, tok=tokens, so=a.so, gain=gain, dy=b.dy, gr=b.gr,
-            segc=segc, segr=segr,
+            kf=a.kf, tab=a.tab, om=om, tok=tokens, so=a.so, gain=gain, dy=b.dy, gr=b.gr,
+            segb=a.segb, segr=segr,
         ),
         (length, width, block, channels, shared, values),
-    )
-    return finish(a, b, c, shared)
+        lax.axis_size("dp"),
+    )
+    return finish(c, shared)
 
 
 def solution(mesh):

time: 373 us -> 265 us (0.71)
  Pallas kernels: 337 us -> 260 us
  other arithmetic: 16.6 us -> 0 us
  local copies, waits for them, and re-layouts: 14 us -> 0 us
    pallas_call x4, Pallas kernels: 337 us -> 260 us  [run_stage(): pl.pallas_call(kernel, out_shape=tuple((jax.ShapeDtypeStruct(shape, kind)...]
    convert_element_type x8 -> x0, other arithmetic: 13.6 us -> none  [the longest x7 12.8 us: finish(): gg, gu, gd, gao, gag, gv, gs, pk = (value.astype(f32) for value in sums)]
    unnamed x27 -> x0, local copies, waits for them, and re-layouts: 6.88 us -> none
where the time goes in v2:
time: 265 us; the launch traced here: 261 us
  Pallas kernels  260 us (98%)
    pallas_call x4, Pallas kernels, run_stage(): pl.pallas_call(kernel, out_shape=tuple((jax.ShapeDtypeStruct(shape, kind)...  260 us

profile of v2, /device:TPU:0, one launch (start us, length us, event | category | flops | bytes accessed | tf_op | source)
XLA Modules:
  0.0 261.3 jit_solution(7573499093729962639)
XLA Ops:
  0.7 72.0 %shard_map.373 = (bf16[1024,1024]{1,0:T(8,128)(2,1)}, f32[2,1024,128]{2,1,0:T(8,128)}, f32[11,16,256]{2,1,0:T(8,128)}, f32[1032,128]{1,0:T(8,128)}, f32[1032,128...) custom-call(bf16[256,1024]{1,0:T(8,128)(2,1)} %refs_30_.1, ...), custom_call_target="tpu_custom_call" | custom-call | tf_op jit(solution)/shard_map/pallas_call | solution.py:131
  72.7 25.3 %shard_map.374 = (bf16[640,1024]{1,0:T(8,128)(2,1)}, bf16[1024,640]{1,0:T(8,128)(2,1)}, bf16[1024,640]{1,0:T(8,128)(2,1)}, f32[256,1024]{1,0:T(8,128)}, f32[1,10...) custom-call(bf16[1024,1024]{1,0:T(8,128)(2,1)} %get-tuple-element.82.refs_0_, ...), custom_call_target="tpu_custom_call" | custom-call | tf_op jit(solution)/shard_map/pallas_call | solution.py:131
  97.9 155.2 %shard_map.375 = (bf16[256,1024]{1,0:T(8,128)(2,1)}, bf16[256,1024]{1,0:T(8,128)(2,1)}, bf16[640,1024]{1,0:T(8,128)(2,1)}, bf16[1024,640]{1,0:T(8,128)(2,1)}, bf...) custom-call(bf16[256,1024]{1,0:T(8,128)(2,1)} %get-tuple-element.86., ...), custom_call_target="tpu_custom_call" | custom-call | tf_op jit(solution)/shard_map/pallas_call | solution.py:131
  253.1 7.9 %shard_map.376 = (f32[16,256]{1,0:T(8,128)}, f32[16,256]{1,0:T(8,128)}, f32[16,256]{1,0:T(8,128)}, f32[16,256]{1,0:T(8,128)}, f32[16,256]{1,0:T(8,128)}, /*index...) custom-call(bf16[256,1024]{1,0:T(8,128)(2,1)} %get-tuple-element.112, ...), custom_call_target="tpu_custom_call" | custom-call | tf_op jit(solution)/shard_map/pallas_call | solution.py:131
